TPU v7x, 256 devices: a whole 4x4x8 slice. The times are simulated.
256 devices in a mesh: pb: 32 (over z_hi, y, x), kv: 8 (over z_lo, core).
Axes of the slice: x: 4, y: 4, z: 8 (z_hi: 2, z_lo: 4; z = z_hi * 4 + z_lo), core: 2. Of those that a mesh axis runs over, the one named last changes fastest.
Arguments:
- queries: bfloat16 [32768, 128], P(('kv', 'pb')), may hold values from -7 to 7
- keys: bfloat16 [32768, 128], P(('kv', 'pb')), may hold values from -7 to 7
- values: bfloat16 [32768, 128], P(('kv', 'pb')), may hold values from -6 to 6
- grad_out: bfloat16 [32768, 128], P(('kv', 'pb')), may hold values from -6 to 6
- block_order: int32 [256], replicated, may hold values from 0 to 255, each once
Outputs:
- attn_out: bfloat16 [32768, 128], P(('kv', 'pb'))
- grad_q: bfloat16 [32768, 128], P(('kv', 'pb'))
- grad_k: bfloat16 [32768, 128], P(('kv', 'pb'))
- grad_v: bfloat16 [32768, 128], P(('kv', 'pb'))
All inputs are finite; a program needn't handle non-finite values.
Results may differ from a plain program's by a relative error of at most 0.029.
Values may be sent and summed in bfloat16 or wider, within the bound.
A program may use at most 256 MiB of HBM per device.

v0:
```python
import jax
import jax.numpy as jnp
from jax import lax
from jax.sharding import PartitionSpec as P

NEG_BIG = -1e30


def combined_all(value, axis, join):
    pieces = jax.tree.map(lambda part: lax.all_gather(part, axis), value)
    head = jax.tree.map(lambda part: part[0], pieces)
    tail = jax.tree.map(lambda part: part[1:], pieces)
    subtotal, _ = lax.scan(lambda subtotal, share: (join(subtotal, share), None), head, tail)
    return subtotal


def score_tile(left, right):
    return lax.dot_general(
        left, right, (((1,), (1,)), ((), ())), preferred_element_type=jnp.float32
    )


def column_tile(left, right):
    return lax.dot_general(
        left, right, (((0,), (0,)), ((), ())), preferred_element_type=jnp.float32
    )


def softmax_combine(first, second):
    upper = jnp.maximum(first[0], second[0])
    scale_one = jnp.exp(first[0] - upper)
    scale_two = jnp.exp(second[0] - upper)
    totals = first[1] * scale_one + second[1] * scale_two
    accums = first[2] * scale_one[:, None] + second[2] * scale_two[:, None]
    return (upper, totals, accums)


def per_device(queries, keys, values, grad_out, block_order):
    n_query = lax.axis_size("pb")
    n_keyval = lax.axis_size("kv")
    pb_index = lax.axis_index("pb")
    kv_index = lax.axis_index("kv")
    tok_rows, head_size = queries.shape
    scale = head_size ** (-0.5)
    offsets = jnp.arange(tok_rows, dtype=jnp.int32)
    query_all, grad_all = (
        lax.all_gather(queries, "kv", axis=0, tiled=True),
        lax.all_gather(grad_out, "kv", axis=0, tiled=True),
    )
    key_all, value_all = (
        lax.all_gather(keys, "pb", axis=0, tiled=True),
        lax.all_gather(values, "pb", axis=0, tiled=True),
    )
    query_ids = jnp.arange(n_keyval, dtype=jnp.int32) * n_query + pb_index
    key_ids = kv_index * n_query + jnp.arange(n_query, dtype=jnp.int32)
    query_pos = (jnp.take(block_order, query_ids)[:, None] * tok_rows + offsets[None, :]).reshape(
        -1
    )
    key_pos = (jnp.take(block_order, key_ids)[:, None] * tok_rows + offsets[None, :]).reshape(-1)
    key_count = key_all.shape[0]
    query_count = query_all.shape[0]
    span = min(512, key_count)
    nblocks = key_count // span
    key_tiles = key_all.reshape(nblocks, span, head_size)
    value_tiles = value_all.reshape(nblocks, span, head_size)
    pos_tiles = key_pos.reshape(nblocks, span)

    def forward_step(carry, inputs):
        run_max, run_total, run_accum = carry
        key_tile, value_tile, tile_pos = inputs
        scores = score_tile(query_all, key_tile) * scale
        allowed = query_pos[:, None] >= tile_pos[None, :]
        new_max = jnp.maximum(run_max, jnp.max(jnp.where(allowed, scores, NEG_BIG), axis=1))
        shrink = jnp.exp(run_max - new_max)
        weights = jnp.where(allowed, jnp.exp(scores - new_max[:, None]), 0.0)
        new_total = run_total * shrink + jnp.sum(weights, axis=1)
        new_accum = run_accum * shrink[:, None] + jnp.dot(
            weights.astype(jnp.bfloat16), value_tile, preferred_element_type=jnp.float32
        )
        return ((new_max, new_total, new_accum), None)

    start = (
        jnp.full((query_count,), NEG_BIG, jnp.float32),
        jnp.zeros((query_count,), jnp.float32),
        jnp.zeros((query_count, head_size), jnp.float32),
    )
    (local_max, local_total, local_accum), unused = lax.scan(
        forward_step, start, (key_tiles, value_tiles, pos_tiles)
    )
    rowmax, total, accum = combined_all(
        (local_max, local_total, local_accum), "kv", softmax_combine
    )
    out_all = (accum / total[:, None]).astype(jnp.bfloat16)
    lse = rowmax + jnp.log(total)
    delta = jnp.sum(grad_all.astype(jnp.float32) * out_all.astype(jnp.float32), axis=1)
    attn_out = lax.dynamic_slice_in_dim(out_all, kv_index * tok_rows, tok_rows, 0)

    def backward_step(carry, inputs):
        key_tile, value_tile, tile_pos = inputs
        scores = score_tile(query_all, key_tile) * scale
        allowed = query_pos[:, None] >= tile_pos[None, :]
        probs = jnp.where(allowed, jnp.exp(scores - lse[:, None]), 0.0)
        dprobs = score_tile(grad_all, value_tile)
        dscores = (probs * (dprobs - delta[:, None])).astype(jnp.bfloat16)
        probs_b = probs.astype(jnp.bfloat16)
        grad_rows = carry + jnp.dot(dscores, key_tile, preferred_element_type=jnp.float32)
        key_terms = column_tile(dscores, query_all) * scale
        value_terms = column_tile(probs_b, grad_all)
        return (grad_rows, jnp.concatenate([key_terms, value_terms], axis=1))

    query_terms, pair_tiles = lax.scan(
        backward_step,
        jnp.zeros((query_count, head_size), jnp.float32),
        (key_tiles, value_tiles, pos_tiles),
    )
    pair_rows = pair_tiles.reshape(key_count, 2 * head_size)
    owned = lax.psum_scatter(pair_rows, "pb", scatter_dimension=0, tiled=True)
    grad_q = lax.psum_scatter(query_terms * scale, "kv", scatter_dimension=0, tiled=True).astype(
        jnp.bfloat16
    )
    grad_k = owned[:, :head_size].astype(jnp.bfloat16)
    grad_v = owned[:, head_size:].astype(jnp.bfloat16)
    return (attn_out, grad_q, grad_k, grad_v)


def solution(mesh):
    in_specs = (
        P(("kv", "pb"), None),
        P(("kv", "pb"), None),
        P(("kv", "pb"), None),
        P(("kv", "pb"), None),
        P(),
    )
    out_specs = (
        P(("kv", "pb"), None),
        P(("kv", "pb"), None),
        P(("kv", "pb"), None),
        P(("kv", "pb"), None),
    )
    return jax.shard_map(
        per_device, mesh=mesh, in_specs=in_specs, out_specs=out_specs, check_vma=False
    )
```

profile of v0, /device:TPU:32, one launch (start us, length us, event | category | flops | bytes accessed | tf_op | source)
XLA Modules:
  0.0 604.6 jit_solution(5055255523050848147)
XLA Ops:
  10.3 15.3 %all_gather.31 = bf16[1024,128]{1,0:T(8,128)(2,1)S(1)} all-gather(bf16[128,128]{1,0:T(8,128)(2,1)} %param.11), channel_id=1, replica_groups=mesh['pb'=32,'kv'=8] {'kv'}, dimensions={0}, use_global_device_ids=true | all-gather | bytes 294912 | tf_op jit(solution)/shard_map/all_gather | solution.py:47
  25.7 68.5 %all-gather.7.cloned.1.call-done = bf16[4096,128]{1,0:T(8,128)(2,1)} async-done(((bf16[128,128]{1,0:T(8,128)(2,1)}), bf16[4096,128]{1,0:T(8,128)(2,1)}) %all-gather.7.cloned.1.call-update) | async-done | bytes 1048592 | tf_op jit(solution)/shard_map/all_gather | solution.py:51
  94.2 79.3 %all-gather.9.cloned.1.call-done = bf16[4096,128]{1,0:T(8,128)(2,1)} async-done(((bf16[128,128]{1,0:T(8,128)(2,1)}), bf16[4096,128]{1,0:T(8,128)(2,1)}) %all-gather.9.cloned.1.call-update) | async-done | bytes 1048592 | tf_op jit(solution)/shard_map/all_gather | solution.py:52
  173.5 31.0 %while.43 = (s32[]{:T(128)}, f32[1024]{0:T(1024)S(1)}, f32[1024]{0:T(1024)S(1)}, f32[1024,128]{1,0:T(8,128)S(1)}, s32[8,512]{1,0:T(8,128)S(1)}, /*index=5*/bf16[...) while((s32[]{:T(128)}, f32[1024]{0:T(1024)S(1)}, ...), condition=%wide.region_3.4_spmd.clone, body=%wide.region_0.3_spmd.clone.sunk | while | flops 276174848 | bytes 7956653 | solution.py:87
  173.6 1.4 fusion.73
  175.5 1.9 convolution_add_fusion.4
  177.5 1.4 fusion.73
  179.4 1.9 convolution_add_fusion.4
  181.4 1.4 fusion.73
  183.3 1.9 convolution_add_fusion.4
  185.2 1.4 fusion.73
  187.1 1.9 convolution_add_fusion.4
  189.1 1.4 fusion.73
  191.0 1.9 convolution_add_fusion.4
  193.0 1.4 fusion.73
  194.9 1.9 convolution_add_fusion.4
  196.9 1.4 fusion.73
  198.8 1.9 convolution_add_fusion.4
  200.8 1.4 fusion.73
  202.7 1.9 convolution_add_fusion.4
  205.5 14.1 %all_gather.39 = bf16[1024,128]{1,0:T(8,128)(2,1)S(1)} all-gather(bf16[128,128]{1,0:T(8,128)(2,1)S(1)} %copy-done.2), channel_id=1, replica_groups=mesh['pb'=32,'kv'=8] {'kv'}, dimensions={0}, use_global_device_ids=true | all-gather | bytes 294912 | tf_op jit(solution)/shard_map/all_gather | solution.py:48
  219.6 14.1 %all-gather = f32[8192]{0:T(1024)S(1)} all-gather(f32[1024]{0:T(1024)S(1)} %get-tuple-element.150), channel_id=2, replica_groups=mesh['pb'=32,'kv'=8] {'kv'}, dimensions={0}, use_global_device_ids=true | all-gather | bytes 36864 | tf_op jit(solution)/shard_map/all_gather | solution.py:10
  233.7 14.0 %all-gather.1 = f32[8192]{0:T(1024)S(1)} all-gather(f32[1024]{0:T(1024)S(1)} %get-tuple-element.151), channel_id=3, replica_groups=mesh['pb'=32,'kv'=8] {'kv'}, dimensions={0}, use_global_device_ids=true | all-gather | bytes 36864 | tf_op jit(solution)/shard_map/all_gather | solution.py:10
  247.7 5.8 all-gather.11.cloned.1.call-done
  253.6 4.1 slice.49
  257.7 10.9 %while.42 = (s32[]{:T(128)}, f32[1024]{0:T(1024)S(1)}, f32[1024]{0:T(1024)S(1)}, f32[1024,128]{1,0:T(8,128)S(1)}, f32[7,1024]{1,0:T(8,128)S(1)}, /*index=5*/f32[...) while((s32[]{:T(128)}, f32[1024]{0:T(1024)S(1)}, f32[1024]{0:T(1024)S(1)}, f32[1024,128]{1,0:T(8,128)S(1)}, ...), condition=%wide.region_5.6_spmd, body=%wide.region_4.5_spmd.sunk | while | flops 399362 | bytes 1630309 | solution.py:13
  257.7 1.5 fusion.69
  259.3 1.5 fusion.69
  260.9 1.5 fusion.69
  262.4 1.5 fusion.69
  264.0 1.5 fusion.69
  265.5 1.5 fusion.69
  267.1 1.5 fusion.69
  269.0 52.4 %while.44 = (s32[]{:T(128)}, f32[1024,128]{1,0:T(8,128)S(1)}, f32[8,512,256]{2,1,0:T(8,128)}, s32[8,512]{1,0:T(8,128)S(1)}, bf16[8,512,128]{2,1,0:T(8,128)(2,1)}...) while((s32[]{:T(128)}, f32[1024,128]{1,0:T(8,128)S(1)}, ...), condition=%wide.region_8.9_spmd.clone, body=%wide.region_7.8_spmd.clone.sunk | while | flops 675742720 | bytes 15620291 | solution.py:111
  269.1 1.5 bitcast_select_fusion.2
  271.1 1.3 fusion.86
  272.9 1.5 convolution_add_fusion.5
  275.6 1.5 bitcast_select_fusion.2
  277.6 1.3 fusion.86
  279.5 1.5 convolution_add_fusion.5
  282.1 1.5 bitcast_select_fusion.2
  284.2 1.3 fusion.86
  286.0 1.5 convolution_add_fusion.5
  287.8 0.9 constant_dynamic-update-slice_fusion.2
  288.7 1.5 bitcast_select_fusion.2
  290.7 1.3 fusion.86
  292.6 1.5 convolution_add_fusion.5
  295.3 1.5 bitcast_select_fusion.2
  297.3 1.3 fusion.86
  299.1 1.5 convolution_add_fusion.5
  301.8 1.5 bitcast_select_fusion.2
  303.8 1.3 fusion.86
  305.6 1.5 convolution_add_fusion.5
  308.3 1.5 bitcast_select_fusion.2
  310.3 1.3 fusion.86
  312.2 1.5 convolution_add_fusion.5
  314.9 1.5 bitcast_select_fusion.2
  316.9 1.3 fusion.86
  318.7 1.5 convolution_add_fusion.5
  321.3 0.8 broadcast_multiply_fusion
  323.4 33.0 %reduce-scatter.3.cloned.1.call-done = f32[128,128]{1,0:T(8,128)} async-done(((f32[1024,128]{1,0:T(8,128)}), f32[128,128]{1,0:T(8,128)}) %reduce-scatter.3.cloned.1.call-update) | async-done | bytes 65552 | tf_op jit(solution)/shard_map/reduce_scatter | solution.py:118
  356.4 1.5 convert_element_type.26
  357.9 238.6 %reduce-scatter.5.cloned.1.call-done = f32[128,256]{1,0:T(8,128)} async-done(((f32[4096,256]{1,0:T(8,128)}), f32[128,256]{1,0:T(8,128)}) %reduce-scatter.5.cloned.1.call-update) | async-done | bytes 131088 | tf_op jit(solution)/shard_map/reduce_scatter | solution.py:117
  596.5 0.9 convert.4
  (162 shorter events, 27.5 us)
Async XLA Ops:
  7.2 1.6 copy-start
  7.2 87.1 %all-gather.7.cloned.1.call-start = ((), (), s32[]{:S(2)}) async-start(), calls=%async_computation.2 | async-start | bytes 1081344 | tf_op jit(solution)/shard_map/all_gather | solution.py:51
  7.9 165.6 %all-gather.9.cloned.1.call-start = ((), (), s32[]{:S(2)}) async-start(), calls=%async_computation.3 | async-start | bytes 1081344 | tf_op jit(solution)/shard_map/all_gather | solution.py:52
  8.7 244.9 %all-gather.11.cloned.1.call-start = ((), (), s32[]{:S(2)}) async-start(), calls=%async_computation.6 | async-start | bytes 4718592 | tf_op jit(solution)/shard_map/all_gather | solution.py:10
  173.5 32.0 %copy-start.2 = (bf16[128,128]{1,0:T(8,128)(2,1)S(1)}, bf16[128,128]{1,0:T(8,128)(2,1)}, u32[]{:S(2)}) copy-start(bf16[128,128]{1,0:T(8,128)(2,1)} %param.14) | copy-start | bytes 98308
  204.6 0.8 copy-start.1
  205.4 151.0 %reduce-scatter.3.cloned.1.call-start = ((), (), s32[]{:S(2)}) async-start(), calls=%async_computation.4 | async-start | bytes 589824 | tf_op jit(solution)/shard_map/reduce_scatter | solution.py:118
  253.6 4.1 slice-start
  322.2 274.3 %reduce-scatter.5.cloned.1.call-start = ((), (), s32[]{:S(2)}) async-start(), calls=%async_computation.5 | async-start | bytes 4325376 | tf_op jit(solution)/shard_map/reduce_scatter | solution.py:117
Sparse Core Ops, SparseCore 0:
  11.4 82.7 all-gather.6
  97.7 75.8 all-gather.8
  205.5 47.9 all-gather.10
  322.3 34.0 reduce-scatter.2
  359.0 237.4 reduce-scatter.4
where the time goes:
time: 606 us; the launch traced here: 605 us
  waiting for transfers between devices  427 us (70%)
  matrix products  68.4 us (11%)
  blocking collectives  57.5 us (9%)
  other arithmetic  20 us (3%)
  local copies, waits for them, and re-layouts  16.3 us (3%)
  between operations  13.9 us (2%)
    reduce_scatter x1, waiting for transfers between devices, per_device(): owned = lax.psum_scatter(pair_rows, 'pb', scatter_dimension=0, tiled=True)  239 us
    all_gather x1, waiting for transfers between devices, per_device(): lax.all_gather(values, 'pb', axis=0, tiled=True)  79.3 us
    all_gather x1, waiting for transfers between devices, per_device(): lax.all_gather(keys, 'pb', axis=0, tiled=True)  68.5 us
    dot_general x24, matrix products, score_tile(): lax.dot_general(left, right, (((1,), (1,)), ((), ())), preferred_element_...  33.6 us
    reduce_scatter x1, waiting for transfers between devices, per_device(): lax.psum_scatter(query_terms * scale, 'kv', scatter_dimension=0, tiled=True)  33 us
    all_gather x2, blocking collectives, combined_all(): pieces = jax.tree.map(lambda part: lax.all_gather(part, axis), value)  28.1 us
    all_gather x1, blocking collectives, per_device(): lax.all_gather(queries, 'kv', axis=0, tiled=True)  15.3 us
    dot_general x8, matrix products, forward_step(): jnp.dot(weights.astype(jnp.bfloat16), value_tile, preferred_element_type=...  14.8 us
  transfers between devices with their start and end apart: 5, of which 5 were waited for; matrix products, arithmetic and copies ran while one was open for 1% of the time, Pallas kernels for 0%

commit v1 on v0

v1 whole, which is shorter than its diff:
```python
import functools

import jax
import jax.numpy as jnp
from jax import lax
from jax.experimental import pallas as pl
from jax.experimental.pallas import tpu as pltpu
from jax.sharding import PartitionSpec as P

MESH = pl.DeviceIdType.MESH
F32 = jnp.float32
BF16 = jnp.bfloat16
BIG = 1e30
B = 128
G = 16
N = B * G
CH = 256
STEPS = N // CH


def dot(left, right, left_dim, right_dim):
    return lax.dot_general(
        left, right, (((left_dim,), (right_dim,)), ((), ())), preferred_element_type=F32
    )


def split3(row):
    first = row.astype(BF16).astype(F32)
    second = (row - first).astype(BF16).astype(F32)
    return [first, second, row - first - second]


def kernel(
    q_ref, k_ref, v_ref, g_ref, order_ref,
    out_ref, dq_ref, dk_ref, dv_ref,
    qg, kvg, kt, vt, bias, tri, stats, probs, dprobs, dsc, o_send, o_recv, st_send, st_recv,
    qs, gs, dq_send, dq_recv, kv_send, kv_recv, ssem, rsem,
):
    scale = B ** -0.5
    log_scale = scale * 1.4426950408889634
    pb, kv = lax.axis_index("pb"), lax.axis_index("kv")
    place = lax.rem(pb, 16)
    x, y = lax.rem(place, 4), place // 4
    z_hi = pb // 16
    z, core = z_hi * 4 + kv // 2, lax.rem(kv, 2)

    def line_peer(slot, sign):
        to_z = lax.rem(z + 8 + sign * (slot // 2), 8)
        to_core = lax.rem(core + lax.rem(slot, 2), 2)
        return (to_z // 4) * 16 + place, lax.rem(to_z, 4) * 2 + to_core

    def plane_peer(slot, sign):
        to_x = lax.rem(x + 4 + sign * lax.rem(slot, 4), 4)
        to_y = lax.rem(y + 4 + sign * (slot // 4), 4)
        return z_hi * 16 + to_y * 4 + to_x, kv

    def copy(kind, src, dst, slot, peer):
        return pltpu.make_async_remote_copy(
            src_ref=src, dst_ref=dst, send_sem=ssem.at[kind, slot], recv_sem=rsem.at[kind, slot],
            device_id=peer, device_id_type=MESH,
        )

    barrier = pltpu.get_barrier_semaphore()

    def greet(slot, carry):
        for peer in (line_peer(slot, 1), plane_peer(slot, 1)):
            pl.semaphore_signal(barrier, inc=1, device_id=peer, device_id_type=MESH)
        return carry

    lax.fori_loop(1, G, greet, 0)
    qg[0, 0] = q_ref[...].T
    qg[0, 1] = g_ref[...].T
    kvg[0, 0] = k_ref[...]
    kvg[0, 1] = v_ref[...]
    pl.semaphore_wait(barrier, 2 * (G - 1))

    def gather_q(slot):
        return copy(0, qg.at[0], qg.at[slot], slot, line_peer(slot, 1))

    def gather_kv(slot):
        return copy(1, kvg.at[0], kvg.at[slot], slot, plane_peer(slot, 1))

    def send_o(slot):
        return copy(2, o_send.at[slot], o_recv.at[slot], slot, line_peer(slot, -1))

    def send_st(slot):
        return copy(3, st_send, st_recv.at[slot], slot, line_peer(slot, 1))

    def send_dq(slot):
        return copy(4, dq_send.at[slot], dq_recv.at[slot], slot, line_peer(slot, -1))

    def send_kv(slot):
        return copy(5, kv_send.at[slot], kv_recv.at[slot], slot, plane_peer(slot, -1))

    def over_slots(*steps):
        def one(slot, carry):
            for step in steps:
                step(slot)
            return carry

        lax.fori_loop(1, G, one, 0)

    over_slots(lambda s: gather_q(s).start(), lambda s: gather_kv(s).start())

    lane = lax.broadcasted_iota(jnp.int32, (B, B), 1)
    sub = lax.broadcasted_iota(jnp.int32, (B, B), 0)
    tri[...] = jnp.zeros_like(tri)
    tri[:, 0:B] = jnp.where(sub > lane, -BIG, 0.0)
    q_pos = []
    for slot in range(G):
        to_pb, to_kv = line_peer(slot, -1)
        q_pos.append(jnp.full((1, B), order_ref[to_kv * 32 + to_pb], jnp.int32))
    q_pos = jnp.concatenate(q_pos, axis=1)
    for slot in range(G):
        to_pb, to_kv = plane_peer(slot, -1)
        bias[slot : slot + 1, :] = jnp.where(order_ref[to_kv * 32 + to_pb] > q_pos, BIG, 0.0)

    over_slots(lambda s: gather_kv(s).wait_recv())

    def turn(slot, carry):
        at = pl.ds(pl.multiple_of(slot * B, B), B)
        kt[:, at] = kvg[slot, 0].T
        vt[:, at] = kvg[slot, 1].T
        return carry

    lax.fori_loop(0, G, turn, 0)
    over_slots(lambda s: gather_q(s).wait_recv())

    def keys():
        return kvg[:, 0].reshape(N, B)

    def values():
        return kvg[:, 1].reshape(N, B)

    def pair(ref, step, which):
        return jnp.concatenate([ref[2 * step, which], ref[2 * step + 1, which]], axis=1)

    def forward(step, carry):
        at = pl.ds(pl.multiple_of(step * CH, CH), CH)
        s = dot(keys(), pair(qg, step, 0), 1, 0).reshape(G, B, CH)
        s = jnp.concatenate([s[0:1] + tri[:, at][None], s[1:]], axis=0)
        off = bias[:, at]
        rowmax = jnp.max(jnp.where(off > 0, -BIG, jnp.max(s, axis=1)), axis=0, keepdims=True)
        shift = jnp.where(off > 0, BIG, rowmax)
        p = jnp.exp2((s - shift[:, None, :]) * log_scale).reshape(N, CH)
        total = jnp.sum(p, axis=0, keepdims=True)
        p = p.astype(BF16)
        probs[:, at] = p
        stats[0:1, at] = rowmax
        accum = dot(vt[...], p, 1, 0)
        rows = split3(rowmax) + split3(total) + [jnp.zeros((10, CH), F32)]
        packed = jnp.concatenate([accum] + rows, axis=0).astype(BF16)
        for half in range(2):
            o_send[2 * step + half] = packed[:, half * B : (half + 1) * B]
        return carry

    lax.fori_loop(0, STEPS, forward, 0)
    over_slots(lambda s: send_o(s).start())

    def dprob(step, carry):
        at = pl.ds(pl.multiple_of(step * CH, CH), CH)
        dprobs[:, at] = dot(values(), pair(qg, step, 1), 1, 0)
        return carry

    lax.fori_loop(0, STEPS, dprob, 0)

    o_recv[0] = o_send[0]
    over_slots(lambda s: send_o(s).wait_recv())
    tail = o_recv[:, B : B + 16].astype(F32)
    maxes = tail[:, 0:1] + tail[:, 1:2] + tail[:, 2:3]
    totals = tail[:, 3:4] + tail[:, 4:5] + tail[:, 5:6]
    top = jnp.max(maxes, axis=0, keepdims=True)
    factor = jnp.exp2((maxes - top) * log_scale)
    whole = jnp.sum(totals * factor, axis=0)
    accum = jnp.zeros((B, B), F32)
    for slot in range(G):
        accum += o_recv[slot, 0:B].astype(F32) * factor[slot]
    out_t = (accum / whole).astype(BF16)
    out_ref[...] = out_t.T
    delta = jnp.sum(qg[0, 1].astype(F32) * out_t.astype(F32), axis=0, keepdims=True)
    lse = top[0] * log_scale + jnp.log2(whole)
    st_send[...] = jnp.concatenate([lse, delta, jnp.zeros((6, B), F32)], axis=0)
    over_slots(lambda s: send_st(s).start())
    st_recv[0] = st_send[...]
    over_slots(lambda s: send_st(s).wait_recv())

    def rescale(slot, carry):
        at = pl.ds(pl.multiple_of(slot * B, B), B)
        weight = jnp.exp2(stats[0:1, at] * log_scale - st_recv[slot, 0:1])
        stats[1:2, at] = st_recv[slot, 1:2]
        stats[2:3, at] = weight * scale
        qs[:, at] = (qg[slot, 0].astype(F32) * weight).astype(BF16)
        gs[:, at] = (qg[slot, 1].astype(F32) * weight).astype(BF16)
        return carry

    lax.fori_loop(0, G, rescale, 0)

    def backward_q(step, carry):
        at = pl.ds(pl.multiple_of(step * CH, CH), CH)
        ds = (probs[:, at].astype(F32) * (dprobs[:, at] - stats[1:2, at])).astype(BF16)
        dsc[:, at] = ds
        terms = (dot(kt[...], ds, 1, 0) * stats[2:3, at]).astype(BF16)
        for half in range(2):
            dq_send[2 * step + half] = terms[:, half * B : (half + 1) * B]
        return carry

    lax.fori_loop(0, STEPS, backward_q, 0)
    over_slots(lambda s: send_dq(s).start())

    def backward_kv(step, carry):
        at = pl.ds(pl.multiple_of(step * CH, CH), CH)
        key_terms = (dot(dsc[at, :], qs[...], 1, 1) * scale).astype(BF16)
        value_terms = dot(probs[at, :], gs[...], 1, 1).astype(BF16)
        for half in range(2):
            kv_send[2 * step + half, 0] = key_terms[half * B : (half + 1) * B]
            kv_send[2 * step + half, 1] = value_terms[half * B : (half + 1) * B]
        return carry

    lax.fori_loop(0, STEPS, backward_kv, 0)
    over_slots(lambda s: send_kv(s).start())

    dq_recv[0] = dq_send[0]
    over_slots(lambda s: send_dq(s).wait_recv())
    dq_ref[...] = jnp.sum(dq_recv[...].astype(F32), axis=0).astype(BF16).T
    kv_recv[0] = kv_send[0]
    over_slots(lambda s: send_kv(s).wait_recv())
    dk_ref[...] = jnp.sum(kv_recv[:, 0].astype(F32), axis=0).astype(BF16)
    dv_ref[...] = jnp.sum(kv_recv[:, 1].astype(F32), axis=0).astype(BF16)
    over_slots(*[lambda s, f=f: f(s).wait_send() for f in (gather_q, gather_kv, send_o, send_st, send_dq, send_kv)])


def per_device(queries, keys, values, grad_out, block_order):
    vmem = pl.BlockSpec(memory_space=pltpu.VMEM)
    block = jax.ShapeDtypeStruct((B, B), BF16)
    return pl.pallas_call(
        kernel,
        out_shape=[block] * 4,
        in_specs=[vmem] * 4 + [pl.BlockSpec(memory_space=pltpu.SMEM)],
        out_specs=[vmem] * 4,
        scratch_shapes=[
            pltpu.VMEM((G, 2, B, B), BF16),
            pltpu.VMEM((G, 2, B, B), BF16),
            pltpu.VMEM((B, N), BF16),
            pltpu.VMEM((B, N), BF16),
            pltpu.VMEM((G, N), F32),
            pltpu.VMEM((B, N), F32),
            pltpu.VMEM((8, N), F32),
            pltpu.VMEM((N, N), BF16),
            pltpu.VMEM((N, N), F32),
            pltpu.VMEM((N, N), BF16),
            pltpu.VMEM((G, B + 16, B), BF16),
            pltpu.VMEM((G, B + 16, B), BF16),
            pltpu.VMEM((8, B), F32),
            pltpu.VMEM((G, 8, B), F32),
            pltpu.VMEM((B, N), BF16),
            pltpu.VMEM((B, N), BF16),
            pltpu.VMEM((G, B, B), BF16),
            pltpu.VMEM((G, B, B), BF16),
            pltpu.VMEM((G, 2, B, B), BF16),
            pltpu.VMEM((G, 2, B, B), BF16),
            pltpu.SemaphoreType.DMA((6, G)),
            pltpu.SemaphoreType.DMA((6, G)),
        ],
        compiler_params=pltpu.CompilerParams(
            collective_id=0, has_side_effects=True, vmem_limit_bytes=60 * 2**20
        ),
        name="attention",
    )(queries, keys, values, grad_out, block_order)


def solution(mesh):
    spec = P(("kv", "pb"), None)
    return jax.shard_map(
        per_device, mesh=mesh, in_specs=(spec, spec, spec, spec, P()), out_specs=(spec,) * 4,
        check_vma=False,
    )
```

time: 606 us -> 101 us (0.17)
  the two profiles are of different devices: /device:TPU:32 before, /device:TPU:1 now
where the time goes in v1:
time: 101 us
  Pallas kernels  96.8 us (96%)
  local copies, waits for them, and re-layouts  3.54 us (4%)
    pallas_call x1, Pallas kernels, per_device(): pl.pallas_call(kernel, out_shape=[block] * 4, in_specs=[vmem] * 4 + [pl.B...  96.8 us
    unnamed x10, local copies, waits for them, and re-layouts  3.54 us

profile of v1, /device:TPU:1, one launch (start us, length us, event | category | flops | bytes accessed | tf_op | source)
XLA Modules:
  0.0 101.0 jit_solution(975116817529819368)
XLA Ops:
  0.6 96.8 %attention.1 = (bf16[128,128]{1,0:T(8,128)(2,1)}, bf16[128,128]{1,0:T(8,128)(2,1)}, bf16[128,128]{1,0:T(8,128)(2,1)}, bf16[128,128]{1,0:T(8,128)(2,1)}) custom-call(bf16[128,128]{1,0:T(8,128)(2,1)} %q_ref.1, bf16[128,128]{1,0:T(8,128)(2,1)} %k_ref.1, bf16[128,128]{1,0:T(8,128)(2,1)} %v_ref.1, bf16[128,128]{1,0:T(8,128)(2,1)} %g_ref.1, s32[256]{0:T(256)} %order_ref.1), custom_call_target="tpu_custom_call" | custom-call | tf_op jit(solution)/shard_map/attention/pallas_call | solution.py:235
  97.5 0.0 copy-start.2
  97.5 1.4 %copy.13 = bf16[128,128]{1,0:T(8,128)(2,1)} copy(bf16[128,128]{1,0:T(8,128)(2,1)} %get-tuple-element.8) | data formatting | bytes 65536
  98.8 0.0 copy-done.2
  98.9 0.0 copy-start.1
  98.9 0.6 copy.14
  99.5 0.2 copy-done.1
  99.6 0.0 copy-start
  99.6 0.6 copy.15
  100.2 0.2 copy-done
  100.4 0.6 copy.16
Async XLA Ops:
  97.5 1.4 %copy-start.2 = (bf16[128,128]{1,0:T(8,128)(2,1)S(1)}, bf16[128,128]{1,0:T(8,128)(2,1)}, u32[]{:S(2)}) copy-start(bf16[128,128]{1,0:T(8,128)(2,1)} %get-tuple-element.9) | copy-start | bytes 98308
  98.9 0.8 copy-start.1
  99.6 0.8 copy-start

commit v2 on v0

v2 whole, which is shorter than its diff:
```python
import jax
import jax.numpy as jnp
from jax import lax
from jax.experimental import pallas as pl
from jax.experimental.pallas import tpu as pltpu
from jax.sharding import PartitionSpec as P

MESH = pl.DeviceIdType.MESH
F32 = jnp.float32
BF16 = jnp.bfloat16
BIG = 1e30
TINY = 1e-30
B = 128
ZQ = 8
NQ = ZQ * B
CHUNKS = 8
KC = 4 * B
CQ = 2 * B
Q_AT, KV_AT, FWD_AT, ST_AT, O_AT, PRE_AT, BACK_AT, DQ_AT, SEMS = 0, 8, 24, 28, 36, 44, 48, 64, 72


def dot(left, right, left_dim, right_dim):
    return lax.dot_general(
        left, right, (((left_dim,), (right_dim,)), ((), ())), preferred_element_type=F32
    )


def ring4(code):
    return code + code // 2 - 2 * (code // 3)


def ring8(code):
    odd = lax.rem(code, 2)
    return odd * ((code + 1) // 2) + (1 - odd) * lax.rem(8 - code // 2, 8)


def kernel(
    q_ref, k_ref, v_ref, g_ref, order_ref,
    out_ref, dq_ref, dk_ref, dv_ref,
    qg, kvg, kt, vt, bias, maxes, totals, deltas, factors, rows, probs, dprobs, dsc,
    st_send, st_recv, o_send, o_recv, pre_send, pre_recv, part, back_send, back_recv, dq_sum, dq_send, dq_recv,
    ssem, rsem,
):
    scale = B ** -0.5
    log_scale = scale * 1.4426950408889634
    pb, kv = lax.axis_index("pb"), lax.axis_index("kv")
    place = lax.rem(pb, 16)
    x, y = lax.rem(place, 4), place // 4
    z_hi = pb // 16
    z, core = z_hi * 4 + kv // 2, lax.rem(kv, 2)

    def line_z(code, sign):
        return lax.rem(z + 8 + sign * ring8(code), 8)

    def line(code, sign):
        to_z = line_z(code, sign)
        return (to_z // 4) * 16 + place, lax.rem(to_z, 4) * 2 + core

    def plane(slot, sign):
        to_x = lax.rem(x + 4 + sign * ring4(lax.rem(slot, 4)), 4)
        to_y = lax.rem(y + 4 + sign * ring4(slot // 4), 4)
        return z_hi * 16 + to_y * 4 + to_x, kv

    sibling = (pb, (kv // 2) * 2 + 1 - core)

    def copy(src, dst, sem, peer):
        return pltpu.make_async_remote_copy(
            src_ref=src, dst_ref=dst, send_sem=ssem.at[sem], recv_sem=rsem.at[sem],
            device_id=peer, device_id_type=MESH,
        )

    def gather_q(i):
        return copy(qg.at[0], qg.at[i], Q_AT + i, line(i, 1))

    def gather_kv(s):
        return copy(kvg.at[0, 0], kvg.at[2 * (s // 4), lax.rem(s, 4)], KV_AT + s, plane(s, 1))

    def forward_kv(t):
        return copy(kvg.at[2 * t], kvg.at[2 * t + 1], FWD_AT + t, sibling)

    def send_st(i):
        return copy(st_send, st_recv.at[z], ST_AT + i, line(i, 1))

    def send_o(i):
        return copy(o_send.at[i], o_recv.at[i], O_AT + i, line(i, -1))

    def send_pre(t):
        return copy(pre_send.at[t], pre_recv.at[t], PRE_AT + t, sibling)

    def send_back(s):
        return copy(back_send.at[s], back_recv.at[s], BACK_AT + s, plane(s, -1))

    def send_dq(i):
        return copy(dq_send.at[i], dq_recv.at[i], DQ_AT + i, line(i, -1))

    def loop(start, stop, *steps):
        def one(i, carry):
            for step in steps:
                step(i)
            return carry

        lax.fori_loop(start, stop, one, 0)

    barrier = pltpu.get_barrier_semaphore()

    def greet(peer):
        pl.semaphore_signal(barrier, inc=1, device_id=peer, device_id_type=MESH)

    loop(1, 16, lambda s: greet(plane(s, 1)))
    loop(1, ZQ, lambda i: greet(line(i, 1)))
    greet(sibling)
    qg[0, 0] = q_ref[...].T
    qg[0, 1] = g_ref[...].T
    kvg[0, 0, 0] = k_ref[...]
    kvg[0, 0, 1] = v_ref[...]
    pl.semaphore_wait(barrier, 15 + ZQ)
    loop(1, ZQ, lambda i: gather_q(i).start(), lambda i: gather_kv(i).start())
    loop(ZQ, 16, lambda s: gather_kv(s).start())

    q_pos = []
    for i in range(ZQ):
        at_pb, at_kv = line(i, -1)
        q_pos.append(jnp.full((1, B), order_ref[at_kv * 32 + at_pb], jnp.int32))
    q_pos = jnp.concatenate(q_pos, axis=1)
    for s in range(16):
        at_pb, at_kv = plane(s, -1)
        for r in range(2):
            k_pos = order_ref[(at_kv + r * (1 - 2 * core)) * 32 + at_pb]
            j, b = 2 * (s // 4) + r, s % 4
            bias[j, b : b + 1, :] = jnp.where(k_pos > q_pos, BIG, 0.0)

    def pair(ref, i, which):
        return jnp.concatenate([ref[2 * i, which], ref[2 * i + 1, which]], axis=1)

    def tile(j, i, own=False):
        at = pl.ds(pl.multiple_of(i * CQ, CQ), CQ)
        s = dot(kvg[j, :, 0].reshape(KC, B), pair(qg, i, 0), 1, 0).reshape(4, B, CQ)
        if own:
            lane = lax.broadcasted_iota(jnp.int32, (B, CQ), 1)
            sub = lax.broadcasted_iota(jnp.int32, (B, CQ), 0)
            later = jnp.where((sub > lane) & (lane < B), -BIG, 0.0)
            s = jnp.concatenate([s[0:1] + later[None], s[1:]], axis=0)
        off = bias[j, :, at] > 0
        rowmax = jnp.max(jnp.where(off, -BIG, jnp.max(s, axis=1)), axis=0, keepdims=True)
        shift = jnp.where(off, BIG, rowmax)
        p = jnp.exp2((s - shift[:, None, :]) * log_scale).reshape(KC, CQ)
        dp = dot(kvg[j, :, 1].reshape(KC, B), pair(qg, i, 1), 1, 0)
        one = pl.ds(j, 1)
        maxes[one, at] = rowmax
        totals[one, at] = jnp.sum(p, axis=0, keepdims=True)
        deltas[one, at] = jnp.sum(p * dp, axis=0, keepdims=True)
        probs[j, :, at] = p.astype(BF16)
        dprobs[j, :, at] = dp

    for t in range(4):
        loop(max(4 * t, 1), 4 * t + 4, lambda s: gather_kv(s).wait_recv())
        forward_kv(t).start()
        loop(max(2 * t, 1), 2 * t + 2, lambda i: gather_q(i).wait_recv())
        if t == 0:
            tile(0, 0, own=True)
        else:
            loop(0, t + 1, lambda i: tile(2 * t, i))
            loop(0, 2 * t, lambda j: tile(j, t))
        forward_kv(t).wait_recv()
        loop(0, t + 1, lambda i: tile(2 * t + 1, i))

    top = jnp.max(maxes[...], axis=0, keepdims=True)
    factor = jnp.exp2((maxes[...] - top) * log_scale)
    total = jnp.maximum(jnp.sum(factor * totals[...], axis=0, keepdims=True), TINY)
    near = top * log_scale + jnp.log2(total)
    mean = jnp.sum(factor * deltas[...], axis=0, keepdims=True) / total
    factors[...] = factor / total
    for i in range(ZQ):
        one = pl.ds(line_z(i, -1), 1)
        st_send[0, one, :] = near[:, i * B : (i + 1) * B]
        st_send[1, one, :] = mean[:, i * B : (i + 1) * B]
    loop(1, ZQ, lambda i: send_st(i).start())
    st_recv[z] = st_send[...]

    def turn(j):
        kt[j] = kvg[j, :, 0].reshape(KC, B).T
        vt[j] = kvg[j, :, 1].reshape(KC, B).T

    loop(0, CHUNKS, turn)

    def attend(i):
        at = pl.ds(pl.multiple_of(i * CQ, CQ), CQ)
        accum = jnp.zeros((B, CQ), F32)
        for j in range(CHUNKS):
            accum += dot(vt[j], probs[j, :, at], 1, 0) * factors[j : j + 1, at]
        accum = accum.astype(BF16)
        o_send[2 * i] = accum[:, :B]
        o_send[2 * i + 1] = accum[:, B:]

    loop(0, ZQ // 2, attend)
    loop(1, ZQ, lambda i: send_o(i).start())
    o_recv[0] = o_send[0]

    loop(1, ZQ, lambda i: send_st(i).wait_recv())
    nears, means = st_recv[:, 0], st_recv[:, 1]
    top = jnp.max(nears, axis=0)
    lse = top + jnp.log2(jnp.sum(jnp.exp2(nears - top[None]), axis=0))
    delta = jnp.sum(jnp.exp2(nears - lse[None]) * means, axis=0)
    rows[0:8, :] = lse
    rows[8:16, :] = delta
    lse_row = jnp.concatenate([rows[pl.ds(line_z(i, -1), 1), :] for i in range(ZQ)], axis=1)
    delta_row = jnp.concatenate([rows[pl.ds(8 + line_z(i, -1), 1), :] for i in range(ZQ)], axis=1)
    maxes[...] = jnp.exp2(maxes[...] * log_scale - lse_row)
    deltas[0:1, :] = delta_row
    dq_sum[...] = jnp.zeros_like(dq_sum)

    def whole(which):
        return jnp.concatenate([qg[i, which] for i in range(ZQ)], axis=1)

    def backward(j):
        for i in range(NQ // CQ):
            at = slice(i * CQ, (i + 1) * CQ)
            p = probs[j, :, at].astype(F32) * maxes[pl.ds(j, 1), at]
            probs[j, :, at] = p.astype(BF16)
            dsc[:, at] = (p * (dprobs[j, :, at] - deltas[0:1, at])).astype(BF16)
        dk = dot(dsc[...], whole(0), 1, 1) * scale
        dv = dot(probs[j], whole(1), 1, 1)
        dq_sum[...] += dot(kt[j], dsc[...], 1, 0)
        return dk.reshape(4, B, B), dv.reshape(4, B, B)

    def merge(t):
        send_pre(t).wait_recv()
        both = (part[t].astype(F32) + pre_recv[t].astype(F32)).astype(BF16)
        back_send[pl.ds(4 * t, 4)] = both
        loop(jnp.maximum(4 * t, 1), 4 * t + 4, lambda s: send_back(s).start())

    def backward_pair(n):
        t = 3 - n
        dk, dv = backward(2 * t + 1)
        pre_send[t, :, 0] = dk.astype(BF16)
        pre_send[t, :, 1] = dv.astype(BF16)
        send_pre(t).start()
        dk, dv = backward(2 * t)
        part[t, :, 0] = dk
        part[t, :, 1] = dv
        merge(t)

    loop(0, 4, backward_pair)
    terms = (dq_sum[...] * scale).astype(BF16)
    for i in range(ZQ):
        dq_send[i] = terms[:, i * B : (i + 1) * B]
    loop(1, ZQ, lambda i: send_dq(i).start())

    loop(1, ZQ, lambda i: send_o(i).wait_recv())
    out = jnp.zeros((B, B), F32)
    for i in range(ZQ):
        weight = jnp.exp2(st_recv[line_z(i, 1), 0, pl.ds(z, 1), :] - rows[pl.ds(z, 1), :])
        out += o_recv[i].astype(F32) * weight
    out_ref[...] = out.astype(BF16).T
    dq_recv[0] = dq_send[0]
    loop(1, ZQ, lambda i: send_dq(i).wait_recv())
    dq_ref[...] = jnp.sum(dq_recv[...].astype(F32), axis=0).astype(BF16).T
    back_recv[0] = back_send[0]
    loop(1, 16, lambda s: send_back(s).wait_recv())
    dk_ref[...] = jnp.sum(back_recv[:, 0].astype(F32), axis=0).astype(BF16)
    dv_ref[...] = jnp.sum(back_recv[:, 1].astype(F32), axis=0).astype(BF16)
    loop(1, ZQ, *[lambda i, f=f: f(i).wait_send() for f in (gather_q, send_st, send_o, send_dq)])
    loop(1, 16, *[lambda s, f=f: f(s).wait_send() for f in (gather_kv, send_back)])
    loop(0, 4, *[lambda t, f=f: f(t).wait_send() for f in (forward_kv, send_pre)])


def per_device(queries, keys, values, grad_out, block_order):
    vmem = pl.BlockSpec(memory_space=pltpu.VMEM)
    block = jax.ShapeDtypeStruct((B, B), BF16)
    return pl.pallas_call(
        kernel,
        out_shape=[block] * 4,
        in_specs=[vmem] * 4 + [pl.BlockSpec(memory_space=pltpu.SMEM)],
        out_specs=[vmem] * 4,
        scratch_shapes=[
            pltpu.VMEM((ZQ, 2, B, B), BF16),
            pltpu.VMEM((CHUNKS, 4, 2, B, B), BF16),
            pltpu.VMEM((CHUNKS, B, KC), BF16),
            pltpu.VMEM((CHUNKS, B, KC), BF16),
            pltpu.VMEM((CHUNKS, 4, NQ), F32),
            pltpu.VMEM((CHUNKS, NQ), F32),
            pltpu.VMEM((CHUNKS, NQ), F32),
            pltpu.VMEM((CHUNKS, NQ), F32),
            pltpu.VMEM((CHUNKS, NQ), F32),
            pltpu.VMEM((16, B), F32),
            pltpu.VMEM((CHUNKS, KC, NQ), BF16),
            pltpu.VMEM((CHUNKS, KC, NQ), F32),
            pltpu.VMEM((KC, NQ), BF16),
            pltpu.VMEM((2, 8, B), F32),
            pltpu.VMEM((ZQ, 2, 8, B), F32),
            pltpu.VMEM((ZQ, B, B), BF16),
            pltpu.VMEM((ZQ, B, B), BF16),
            pltpu.VMEM((4, 4, 2, B, B), BF16),
            pltpu.VMEM((4, 4, 2, B, B), BF16),
            pltpu.VMEM((4, 4, 2, B, B), F32),
            pltpu.VMEM((16, 2, B, B), BF16),
            pltpu.VMEM((16, 2, B, B), BF16),
            pltpu.VMEM((B, NQ), F32),
            pltpu.VMEM((ZQ, B, B), BF16),
            pltpu.VMEM((ZQ, B, B), BF16),
            pltpu.SemaphoreType.DMA((SEMS,)),
            pltpu.SemaphoreType.DMA((SEMS,)),
        ],
        compiler_params=pltpu.CompilerParams(
            collective_id=0, has_side_effects=True, vmem_limit_bytes=60 * 2**20
        ),
        name="attention",
    )(queries, keys, values, grad_out, block_order)


def solution(mesh):
    spec = P(("kv", "pb"), None)
    return jax.shard_map(
        per_device, mesh=mesh, in_specs=(spec, spec, spec, spec, P()), out_specs=(spec,) * 4,
        check_vma=False,
    )
```

time: 606 us -> 66.5 us (0.11)
  the two profiles are of different devices: /device:TPU:32 before, /device:TPU:1 now
where the time goes in v2:
time: 66.5 us; the launch traced here: 66.1 us
  Pallas kernels  61.9 us (93%)
  local copies, waits for them, and re-layouts  3.54 us (5%)
    pallas_call x1, Pallas kernels, per_device(): pl.pallas_call(kernel, out_shape=[block] * 4, in_specs=[vmem] * 4 + [pl.B...  61.9 us
    unnamed x10, local copies, waits for them, and re-layouts  3.54 us

profile of v2, /device:TPU:1, one launch (start us, length us, event | category | flops | bytes accessed | tf_op | source)
XLA Modules:
  0.0 66.1 jit_solution(12753894483371568303)
XLA Ops:
  0.6 61.9 %attention.1 = (bf16[128,128]{1,0:T(8,128)(2,1)}, bf16[128,128]{1,0:T(8,128)(2,1)}, bf16[128,128]{1,0:T(8,128)(2,1)}, bf16[128,128]{1,0:T(8,128)(2,1)}) custom-call(bf16[128,128]{1,0:T(8,128)(2,1)} %q_ref.1, bf16[128,128]{1,0:T(8,128)(2,1)} %k_ref.1, bf16[128,128]{1,0:T(8,128)(2,1)} %v_ref.1, bf16[128,128]{1,0:T(8,128)(2,1)} %g_ref.1, s32[256]{0:T(256)} %order_ref.1), custom_call_target="tpu_custom_call" | custom-call | tf_op jit(solution)/shard_map/attention/pallas_call | solution.py:270
  62.6 0.0 copy-start.2
  62.6 1.4 %copy.13 = bf16[128,128]{1,0:T(8,128)(2,1)} copy(bf16[128,128]{1,0:T(8,128)(2,1)} %get-tuple-element.8) | data formatting | bytes 65536
  63.9 0.0 copy-done.2
  63.9 0.0 copy-start.1
  63.9 0.6 copy.14
  64.6 0.2 copy-done.1
  64.7 0.0 copy-start
  64.7 0.6 copy.15
  65.3 0.2 copy-done
  65.5 0.6 copy.16
Async XLA Ops:
  62.6 1.4 %copy-start.2 = (bf16[128,128]{1,0:T(8,128)(2,1)S(1)}, bf16[128,128]{1,0:T(8,128)(2,1)}, u32[]{:S(2)}) copy-start(bf16[128,128]{1,0:T(8,128)(2,1)} %get-tuple-element.9) | copy-start | bytes 98308
  63.9 0.8 %copy-start.1 = (bf16[128,128]{1,0:T(8,128)(2,1)S(1)}, bf16[128,128]{1,0:T(8,128)(2,1)}, u32[]{:S(2)}) copy-start(bf16[128,128]{1,0:T(8,128)(2,1)} %get-tuple-element.10) | copy-start | bytes 98308
  64.7 0.8 %copy-start = (bf16[128,128]{1,0:T(8,128)(2,1)S(1)}, bf16[128,128]{1,0:T(8,128)(2,1)}, u32[]{:S(2)}) copy-start(bf16[128,128]{1,0:T(8,128)(2,1)} %get-tuple-element.11) | copy-start | bytes 98308

commit v3 on v2

v3 whole, which is shorter than its diff:
```python
import jax
import jax.numpy as jnp
from jax import lax
from jax.experimental import pallas as pl
from jax.experimental.pallas import tpu as pltpu
from jax.sharding import PartitionSpec as P

MESH = pl.DeviceIdType.MESH
F32 = jnp.float32
BF16 = jnp.bfloat16
BIG = 1e30
TINY = 1e-30
B = 128
ZQ = 8
NQ = ZQ * B
CHUNKS = 8
KC = 4 * B
CQ = 2 * B
RING4 = (0, 1, 3, 2)
RING8 = (0, 1, 7, 2, 6, 3, 5, 4)


class Sems:
    def __init__(self):
        self.count = 0

    def take(self):
        self.count += 1
        return self.count - 1


SEMS = 82

def dot(left, right, left_dim, right_dim):
    return lax.dot_general(
        left, right, (((left_dim,), (right_dim,)), ((), ())), preferred_element_type=F32
    )


def kernel(
    q_ref, k_ref, v_ref, g_ref, order_ref,
    out_ref, dq_ref, dk_ref, dv_ref,
    qg, kvg, kt, vt, bias, maxes, totals, deltas, factors, rows, probs, dprobs, dscores,
    st_send, st_recv, o_send, o_recv, dq_send, dq_recv, pre_send, pre_recv, part,
    dk_row, dk_got, dk_turn, dk_last, dv_col, dv_got, dv_turn, dv_last,
    ssem, rsem,
):
    scale = B ** -0.5
    log_scale = scale * 1.4426950408889634
    pb, kv = lax.axis_index("pb"), lax.axis_index("kv")
    place = lax.rem(pb, 16)
    x, y = lax.rem(place, 4), place // 4
    z_hi = pb // 16
    z, core = z_hi * 4 + kv // 2, lax.rem(kv, 2)

    xs = [lax.rem(x + d, 4) for d in range(4)]
    ys = [lax.rem(y + d, 4) for d in range(4)]
    zs = [lax.rem(z + d, 8) for d in range(8)]
    pb_z = [at // 4 * 16 + place for at in zs]
    kv_z = [lax.rem(at, 4) * 2 + core for at in zs]

    def row(dx):
        return (z_hi * 16 + y * 4 + xs[dx % 4], kv)

    def column(dy):
        return (z_hi * 16 + ys[dy % 4] * 4 + x, kv)

    def line(dz):
        return (pb_z[dz % 8], kv_z[dz % 8])

    sibling = (pb, kv + 1 - 2 * core)
    sems = Sems()

    def copy(src, dst, peer):
        at = sems.take()
        return pltpu.make_async_remote_copy(
            src_ref=src, dst_ref=dst, send_sem=ssem.at[at], recv_sem=rsem.at[at],
            device_id=peer, device_id_type=MESH,
        )

    sent = []

    def start(copies):
        for one in copies:
            one.start()
            sent.append(one)

    def arrived(copies):
        for one in copies:
            one.wait_recv()

    barrier = pltpu.get_barrier_semaphore()
    peers = [line(d) for d in range(1, 8)] + [f(d) for f in (row, column) for d in (1, 2, 3)] + [sibling]
    for peer in peers:
        pl.semaphore_signal(barrier, inc=1, device_id=peer, device_id_type=MESH)
    qg[0, 0] = q_ref[...].T
    qg[0, 1] = g_ref[...].T
    kvg[0, 0, 0, 0] = k_ref[...]
    kvg[0, 0, 1, 0] = v_ref[...]
    pl.semaphore_wait(barrier, len(peers))

    k_row = {b: copy(kvg.at[0, 0, 0, 0], kvg.at[0, 0, 0, b], row(RING4[b])) for b in (1, 2, 3)}
    v_col = {t: copy(kvg.at[0, 0, 1, 0], kvg.at[t, 0, 1, 0], column(RING4[t])) for t in (1, 2, 3)}
    q_near = {i: copy(qg.at[0], qg.at[i], line(RING8[i])) for i in (3, 4, 1, 2)}
    k_col = {t: copy(kvg.at[0, 0, 0, 0], kvg.at[t, 0, 0, 0], column(RING4[t])) for t in (1, 2, 3)}
    v_row = {b: copy(kvg.at[0, 0, 1, 0], kvg.at[0, 0, 1, b], row(RING4[b])) for b in (1, 2, 3)}
    k_on = {t: copy(kvg.at[0, 0, 0, pl.ds(1, 3)], kvg.at[t, 0, 0, pl.ds(1, 3)], column(RING4[t])) for t in (1, 2, 3)}
    v_on = {
        t: [copy(kvg.at[t, 0, 1, 0], kvg.at[t, 0, 1, b], row(RING4[b])) for b in (1, 2, 3)] for t in (1, 2, 3)
    }
    q_on = {
        5: [copy(qg.at[3], qg.at[5], line(1))],
        6: [copy(qg.at[4], qg.at[6], line(-1))],
        7: [copy(qg.at[3, 0], qg.at[7, 0], line(2)), copy(qg.at[4, 1], qg.at[7, 1], line(-2))],
    }
    share = [copy(kvg.at[t, 0], kvg.at[t, 1], sibling) for t in range(4)]

    start(k_row.values())
    start(v_col.values())
    start(q_near.values())
    start(k_col.values())
    start(v_row.values())

    q_pos = []
    for i in range(ZQ):
        at_pb, at_kv = line(-RING8[i])
        q_pos.append(jnp.full((1, B), order_ref[at_kv * 32 + at_pb], jnp.int32))
    q_pos = jnp.concatenate(q_pos, axis=1)
    for t in range(4):
        for b in range(4):
            at_pb = z_hi * 16 + ys[-RING4[t] % 4] * 4 + xs[-RING4[b] % 4]
            for r in range(2):
                k_pos = order_ref[(kv + r * (1 - 2 * core)) * 32 + at_pb]
                bias[2 * t + r, b : b + 1, :] = jnp.where(k_pos > q_pos, BIG, 0.0)

    def pair(i, which):
        return jnp.concatenate([qg[2 * i, which], qg[2 * i + 1, which]], axis=1)

    def chunk(t, r, which):
        return kvg[t, r, which].reshape(KC, B)

    def tile(t, r, i, own=False):
        j = 2 * t + r
        at = pl.ds(pl.multiple_of(i * CQ, CQ), CQ)
        s = dot(chunk(t, r, 0), pair(i, 0), 1, 0).reshape(4, B, CQ)
        if own:
            lane = lax.broadcasted_iota(jnp.int32, (B, CQ), 1)
            sub = lax.broadcasted_iota(jnp.int32, (B, CQ), 0)
            later = jnp.where((sub > lane) & (lane < B), -BIG, 0.0)
            s = jnp.concatenate([s[0:1] + later[None], s[1:]], axis=0)
        off = bias[j, :, at] > 0
        rowmax = jnp.max(jnp.where(off, -BIG, jnp.max(s, axis=1)), axis=0, keepdims=True)
        shift = jnp.where(off, BIG, rowmax)
        p = jnp.exp2((s - shift[:, None, :]) * log_scale).reshape(KC, CQ)
        dp = dot(chunk(t, r, 1), pair(i, 1), 1, 0)
        one = pl.ds(j, 1)
        maxes[one, at] = rowmax
        totals[one, at] = jnp.sum(p, axis=0, keepdims=True)
        deltas[one, at] = jnp.sum(p * dp, axis=0, keepdims=True)
        probs[j, :, at] = p.astype(BF16)
        dprobs[j, :, at] = dp

    def loop(start, stop, step):
        def one(i, carry):
            step(i)
            return carry

        lax.fori_loop(start, stop, one, 0)

    def tiles_by_query(t, r, stop):
        loop(0, stop, lambda i: tile(t, r, i))

    def tiles_by_chunk(stop, i):
        loop(0, stop, lambda j: tile(j // 2, lax.rem(j, 2), i))

    def key_row(t):
        arrived([k_col[t], k_on[t]] + v_on[t])
        start([share[t]])

    arrived(k_row.values())
    start(k_on.values())
    arrived(v_col.values())
    for t in (1, 2, 3):
        start(v_on[t])
    arrived([q_near[3], q_near[4]])
    for i in (5, 6, 7):
        start(q_on[i])
    arrived(v_row.values())
    start([share[0]])
    arrived([q_near[1], q_near[2]])
    tile(0, 0, 0, own=True)
    tile(0, 0, 1)
    arrived([share[0]])
    tiles_by_query(0, 1, 2)
    key_row(1)
    tiles_by_query(1, 0, 2)
    key_row(2)
    arrived([share[1]])
    tiles_by_query(1, 1, 2)
    arrived(q_on[5])
    key_row(3)
    tiles_by_chunk(4, 2)
    arrived([share[2]])
    loop(0, 3, lambda i: [tile(2, 0, i), tile(2, 1, i)])
    arrived(q_on[6] + q_on[7])
    tiles_by_chunk(6, 3)
    arrived([share[3]])
    loop(0, 4, lambda i: [tile(3, 0, i), tile(3, 1, i)])

    top = jnp.max(maxes[...], axis=0, keepdims=True)
    factor = jnp.exp2((maxes[...] - top) * log_scale)
    total = jnp.maximum(jnp.sum(factor * totals[...], axis=0, keepdims=True), TINY)
    near = top * log_scale + jnp.log2(total)
    mean = jnp.sum(factor * deltas[...], axis=0, keepdims=True) / total
    factors[...] = factor / total
    for i in range(ZQ):
        one = pl.ds(zs[-RING8[i] % 8], 1)
        st_send[0, one, :] = near[:, i * B : (i + 1) * B]
        st_send[1, one, :] = mean[:, i * B : (i + 1) * B]
    stats = [copy(st_send, st_recv.at[z], line(RING8[i])) for i in range(1, ZQ)]
    start(stats)
    st_recv[z] = st_send[...]

    def turn(j):
        t, r = j // 2, lax.rem(j, 2)
        kt[j] = chunk(t, r, 0).T
        vt[j] = chunk(t, r, 1).T

    loop(0, CHUNKS, turn)

    def attend(i):
        at = pl.ds(pl.multiple_of(i * CQ, CQ), CQ)
        accum = jnp.zeros((B, CQ), F32)
        for j in range(CHUNKS):
            accum += dot(vt[j], probs[j, :, at], 1, 0) * factors[j : j + 1, at]
        accum = accum.astype(BF16)
        o_send[2 * i] = accum[:, :B]
        o_send[2 * i + 1] = accum[:, B:]

    loop(0, ZQ // 2, attend)
    o_copies = [copy(o_send.at[i], o_recv.at[i], line(-RING8[i])) for i in range(1, ZQ)]
    start(o_copies)
    o_recv[0] = o_send[0]

    arrived(stats)
    nears, means = st_recv[:, 0], st_recv[:, 1]
    top = jnp.max(nears, axis=0)
    lse = top + jnp.log2(jnp.sum(jnp.exp2(nears - top[None]), axis=0))
    rows[0:8, :] = lse
    rows[8:16, :] = jnp.sum(jnp.exp2(nears - lse[None]) * means, axis=0)

    def row_of(first):
        return jnp.concatenate([rows[pl.ds(first + zs[-RING8[i] % 8], 1), :] for i in range(ZQ)], axis=1)

    maxes[...] = jnp.exp2(maxes[...] * log_scale - row_of(0))
    deltas[0:1, :] = row_of(8)

    def backward_q(i):
        at = pl.ds(pl.multiple_of(i * CQ, CQ), CQ)
        accum = jnp.zeros((B, CQ), F32)
        for j in range(CHUNKS):
            p = probs[j, :, at].astype(F32) * maxes[j : j + 1, at]
            probs[j, :, at] = p.astype(BF16)
            ds = (p * (dprobs[j, :, at] - deltas[0:1, at])).astype(BF16)
            dscores[j, :, at] = ds
            accum += dot(kt[j], ds, 1, 0)
        accum = (accum * scale).astype(BF16)
        dq_send[2 * i] = accum[:, :B]
        dq_send[2 * i + 1] = accum[:, B:]

    dq_copies = [copy(dq_send.at[i], dq_recv.at[i], line(-RING8[i])) for i in range(1, ZQ)]
    loop(0, ZQ // 2, backward_q)
    start(dq_copies)
    dq_recv[0] = dq_send[0]

    def whole(which):
        return jnp.concatenate([qg[i, which] for i in range(ZQ)], axis=1)

    def key_terms(t, r):
        j = 2 * t + r
        dk = dot(dscores[j], whole(0), 1, 1) * scale
        dv = dot(probs[j], whole(1), 1, 1)
        return dk.reshape(4, B, B), dv.reshape(4, B, B)

    swap = {t: copy(pre_send.at[t], pre_recv.at[t], sibling) for t in range(4)}
    dk_out = {t: copy(dk_row.at[t], dk_got.at[t], column(-RING4[t])) for t in (1, 2, 3)}
    dv_out = {
        t: [copy(dv_col.at[t, b], dv_got.at[t, b], row(-RING4[b])) for b in (1, 2, 3)] for t in range(4)
    }
    dk_end = {b: copy(dk_turn.at[b], dk_last.at[b], row(-RING4[b])) for b in (1, 2, 3)}
    dv_end = {t: copy(dv_turn.at[t], dv_last.at[t], column(-RING4[t])) for t in (1, 2, 3)}

    def key_grads(t):
        dk, dv = key_terms(t, 1)
        pre_send[t, 0] = dk.astype(BF16)
        pre_send[t, 1] = dv.astype(BF16)
        start([swap[t]])
        dk, dv = key_terms(t, 0)
        part[0] = dk
        part[1] = dv
        arrived([swap[t]])
        dk_row[t] = (part[0] + pre_recv[t, 0].astype(F32)).astype(BF16)
        dv_col[t] = (part[1] + pre_recv[t, 1].astype(F32)).astype(BF16)
        if t:
            start([dk_out[t]])
        start(dv_out[t])

    def column_sum(t):
        arrived(dv_out[t])
        whole_sum = dv_col[t, 0].astype(F32)
        for b in (1, 2, 3):
            whole_sum += dv_got[t, b].astype(F32)
        return whole_sum

    def dv_pass(t):
        dv_turn[t] = column_sum(t).astype(BF16)
        start([dv_end[t]])

    key_grads(3)
    key_grads(2)
    key_grads(1)
    dv_pass(3)
    key_grads(0)
    arrived(dk_out.values())
    turned = dk_row[0].astype(F32)
    for t in (1, 2, 3):
        turned += dk_got[t].astype(F32)
    dk_turn[...] = turned.astype(BF16)
    start(dk_end.values())
    dv_pass(2)
    dv_pass(1)

    arrived(o_copies)
    out = jnp.zeros((B, B), F32)
    for i in range(ZQ):
        weight = jnp.exp2(st_recv[zs[RING8[i]], 0, pl.ds(z, 1), :] - rows[pl.ds(z, 1), :])
        out += o_recv[i].astype(F32) * weight
    out_ref[...] = out.astype(BF16).T
    arrived(dq_copies)
    dq_ref[...] = jnp.sum(dq_recv[...].astype(F32), axis=0).astype(BF16).T
    total_v = column_sum(0)
    arrived(dv_end.values())
    for t in (1, 2, 3):
        total_v += dv_last[t].astype(F32)
    dv_ref[...] = total_v.astype(BF16)
    total_k = dk_turn[0].astype(F32)
    arrived(dk_end.values())
    for b in (1, 2, 3):
        total_k += dk_last[b].astype(F32)
    dk_ref[...] = total_k.astype(BF16)
    for one in sent:
        one.wait_send()


def finish(a_ref, b_ref, c_ref, d_ref, *outs):
    for src, dst in zip((a_ref, b_ref, c_ref, d_ref), outs):
        dst[...] = src[...]


def per_device(queries, keys, values, grad_out, block_order):
    vmem = pl.BlockSpec(memory_space=pltpu.VMEM)
    block = jax.ShapeDtypeStruct((B, B), BF16)
    parts = pl.pallas_call(
        kernel,
        out_shape=[block] * 4,
        in_specs=[vmem] * 4 + [pl.BlockSpec(memory_space=pltpu.SMEM)],
        out_specs=[vmem] * 4,
        scratch_shapes=[
            pltpu.VMEM((ZQ, 2, B, B), BF16),
            pltpu.VMEM((4, 2, 2, 4, B, B), BF16),
            pltpu.VMEM((CHUNKS, B, KC), BF16),
            pltpu.VMEM((CHUNKS, B, KC), BF16),
            pltpu.VMEM((CHUNKS, 4, NQ), F32),
            pltpu.VMEM((CHUNKS, NQ), F32),
            pltpu.VMEM((CHUNKS, NQ), F32),
            pltpu.VMEM((CHUNKS, NQ), F32),
            pltpu.VMEM((CHUNKS, NQ), F32),
            pltpu.VMEM((16, B), F32),
            pltpu.VMEM((CHUNKS, KC, NQ), BF16),
            pltpu.VMEM((CHUNKS, KC, NQ), F32),
            pltpu.VMEM((CHUNKS, KC, NQ), BF16),
            pltpu.VMEM((2, 8, B), F32),
            pltpu.VMEM((ZQ, 2, 8, B), F32),
            pltpu.VMEM((ZQ, B, B), BF16),
            pltpu.VMEM((ZQ, B, B), BF16),
            pltpu.VMEM((ZQ, B, B), BF16),
            pltpu.VMEM((ZQ, B, B), BF16),
            pltpu.VMEM((4, 2, 4, B, B), BF16),
            pltpu.VMEM((4, 2, 4, B, B), BF16),
            pltpu.VMEM((2, 4, B, B), F32),
            pltpu.VMEM((4, 4, B, B), BF16),
            pltpu.VMEM((4, 4, B, B), BF16),
            pltpu.VMEM((4, B, B), BF16),
            pltpu.VMEM((4, B, B), BF16),
            pltpu.VMEM((4, 4, B, B), BF16),
            pltpu.VMEM((4, 4, B, B), BF16),
            pltpu.VMEM((4, B, B), BF16),
            pltpu.VMEM((4, B, B), BF16),
            pltpu.SemaphoreType.DMA((SEMS,)),
            pltpu.SemaphoreType.DMA((SEMS,)),
        ],
        compiler_params=pltpu.CompilerParams(
            collective_id=0, has_side_effects=True, vmem_limit_bytes=60 * 2**20
        ),
        name="attention",
    )(queries, keys, values, grad_out, block_order)
    return pl.pallas_call(
        finish, out_shape=[block] * 4, in_specs=[vmem] * 4, out_specs=[vmem] * 4, name="finish"
    )(*parts)


def solution(mesh):
    spec = P(("kv", "pb"), None)
    return jax.shard_map(
        per_device, mesh=mesh, in_specs=(spec, spec, spec, spec, P()), out_specs=(spec,) * 4,
        check_vma=False,
    )
```

time: 66.5 us -> 60.3 us (0.907)
  local copies, waits for them, and re-layouts: 3.54 us -> 0 us
  Pallas kernels: 61.9 us -> 59.4 us
    pallas_call x1, Pallas kernels: 61.9 us -> 58 us  [per_device(): pl.pallas_call(kernel, out_shape=[block] * 4, in_specs=[vmem] * 4 + [pl.B...]
    unnamed x10 -> x0, local copies, waits for them, and re-layouts: 3.54 us -> none
    pallas_call x0 -> x1, Pallas kernels: none -> 1.46 us  [per_device(): pl.pallas_call(finish, out_shape=[block] * 4, in_specs=[vmem] * 4, out_sp...]
where the time goes in v3:
time: 60.3 us; the launch traced here: 60.1 us
  Pallas kernels  59.4 us (99%)
  between operations  0.64 us (1%)
    pallas_call x1, Pallas kernels, per_device(): pl.pallas_call(kernel, out_shape=[block] * 4, in_specs=[vmem] * 4 + [pl.B...  58 us
    pallas_call x1, Pallas kernels, per_device(): pl.pallas_call(finish, out_shape=[block] * 4, in_specs=[vmem] * 4, out_sp...  1.46 us

profile of v3, /device:TPU:1, one launch (start us, length us, event | category | flops | bytes accessed | tf_op | source)
XLA Modules:
  0.0 60.1 jit_solution(17403036464132922517)
XLA Ops:
  0.6 58.0 %attention.1 = (bf16[128,128]{1,0:T(8,128)(2,1)}, bf16[128,128]{1,0:T(8,128)(2,1)}, bf16[128,128]{1,0:T(8,128)(2,1)}, bf16[128,128]{1,0:T(8,128)(2,1)}) custom-call(bf16[128,128]{1,0:T(8,128)(2,1)} %q_ref.1, bf16[128,128]{1,0:T(8,128)(2,1)} %k_ref.1, bf16[128,128]{1,0:T(8,128)(2,1)} %v_ref.1, bf16[128,128]{1,0:T(8,128)(2,1)} %g_ref.1, s32[256]{0:T(256)} %order_ref.1), custom_call_target="tpu_custom_call" | custom-call | tf_op jit(solution)/shard_map/attention/pallas_call | solution.py:363
  58.6 1.5 %finish.1 = (bf16[128,128]{1,0:T(8,128)(2,1)}, bf16[128,128]{1,0:T(8,128)(2,1)}, bf16[128,128]{1,0:T(8,128)(2,1)}, bf16[128,128]{1,0:T(8,128)(2,1)}) custom-call(bf16[128,128]{1,0:T(8,128)(2,1)} %get-tuple-element.8.a_ref, bf16[128,128]{1,0:T(8,128)(2,1)} %get-tuple-element.9.b_ref, bf16[128,128]{1,0:T(8,128)(2,1)} %get-tuple-element.10.c_ref, ...), custom_call_target="tpu_custom_call" | custom-call | tf_op jit(solution)/shard_map/finish/pallas_call | solution.py:407

commit v4 on v3

--- a/solution.py
+++ b/solution.py
@@ -15,7 +15,7 @@
 NQ = ZQ * B
 CHUNKS = 8
 KC = 4 * B
-CQ = 2 * B
+CH = 4 * B
 RING4 = (0, 1, 3, 2)
 RING8 = (0, 1, 7, 2, 6, 3, 5, 4)
 
@@ -40,7 +40,7 @@
 def kernel(
     q_ref, k_ref, v_ref, g_ref, order_ref,
     out_ref, dq_ref, dk_ref, dv_ref,
-    qg, kvg, kt, vt, bias, maxes, totals, deltas, factors, rows, probs, dprobs, dscores,
+    qg, kvg, kt, vt, bias, maxes, totals, deltas, factors, rowdelta, rows, probs, dprobs, dscores,
     st_send, st_recv, o_send, o_recv, dq_send, dq_recv, pre_send, pre_recv, part,
     dk_row, dk_got, dk_turn, dk_last, dv_col, dv_got, dv_turn, dv_last,
     ssem, rsem,
@@ -133,31 +133,31 @@
                 k_pos = order_ref[(kv + r * (1 - 2 * core)) * 32 + at_pb]
                 bias[2 * t + r, b : b + 1, :] = jnp.where(k_pos > q_pos, BIG, 0.0)
 
-    def pair(i, which):
-        return jnp.concatenate([qg[2 * i, which], qg[2 * i + 1, which]], axis=1)
+    def quad(half, which):
+        return jnp.concatenate([qg[4 * half + i, which] for i in range(4)], axis=1)
 
     def chunk(t, r, which):
         return kvg[t, r, which].reshape(KC, B)
 
-    def tile(t, r, i, own=False):
+    def unit(t, r, half, own=False):
         j = 2 * t + r
-        at = pl.ds(pl.multiple_of(i * CQ, CQ), CQ)
-        s = dot(chunk(t, r, 0), pair(i, 0), 1, 0).reshape(4, B, CQ)
-        if own:
-            lane = lax.broadcasted_iota(jnp.int32, (B, CQ), 1)
-            sub = lax.broadcasted_iota(jnp.int32, (B, CQ), 0)
-            later = jnp.where((sub > lane) & (lane < B), -BIG, 0.0)
-            s = jnp.concatenate([s[0:1] + later[None], s[1:]], axis=0)
-        off = bias[j, :, at] > 0
-        rowmax = jnp.max(jnp.where(off, -BIG, jnp.max(s, axis=1)), axis=0, keepdims=True)
-        shift = jnp.where(off, BIG, rowmax)
-        p = jnp.exp2((s - shift[:, None, :]) * log_scale).reshape(KC, CQ)
-        dp = dot(chunk(t, r, 1), pair(i, 1), 1, 0)
-        one = pl.ds(j, 1)
-        maxes[one, at] = rowmax
-        totals[one, at] = jnp.sum(p, axis=0, keepdims=True)
-        deltas[one, at] = jnp.sum(p * dp, axis=0, keepdims=True)
-        probs[j, :, at] = p.astype(BF16)
+        at = slice(half * CH, (half + 1) * CH)
+        s = dot(chunk(t, r, 0), quad(half, 0), 1, 0)
+        dp = dot(chunk(t, r, 1), quad(half, 1), 1, 0)
+        for b in range(4):
+            here = slice(b * B, (b + 1) * B)
+            sb, db = s[here], dp[here]
+            if own and b == 0:
+                lane = lax.broadcasted_iota(jnp.int32, (B, B), 1)
+                sub = lax.broadcasted_iota(jnp.int32, (B, B), 0)
+                first = sb[:, :B] + jnp.where(sub > lane, -BIG, 0.0)
+                sb = jnp.concatenate([first, sb[:, B:]], axis=1)
+            top = jnp.max(sb, axis=0, keepdims=True)
+            p = jnp.exp2((sb - top) * log_scale)
+            maxes[j, b : b + 1, at] = top
+            totals[j, b : b + 1, at] = jnp.sum(p, axis=0, keepdims=True)
+            deltas[j, b : b + 1, at] = jnp.sum(p * db, axis=0, keepdims=True)
+            probs[j, here, at] = p.astype(BF16)
         dprobs[j, :, at] = dp
 
     def loop(start, stop, step):
@@ -166,12 +166,6 @@
             return carry
 
         lax.fori_loop(start, stop, one, 0)
-
-    def tiles_by_query(t, r, stop):
-        loop(0, stop, lambda i: tile(t, r, i))
-
-    def tiles_by_chunk(stop, i):
-        loop(0, stop, lambda j: tile(j // 2, lax.rem(j, 2), i))
 
     def key_row(t):
         arrived([k_col[t], k_on[t]] + v_on[t])
@@ -188,30 +182,24 @@
     arrived(v_row.values())
     start([share[0]])
     arrived([q_near[1], q_near[2]])
-    tile(0, 0, 0, own=True)
-    tile(0, 0, 1)
-    arrived([share[0]])
-    tiles_by_query(0, 1, 2)
-    key_row(1)
-    tiles_by_query(1, 0, 2)
-    key_row(2)
-    arrived([share[1]])
-    tiles_by_query(1, 1, 2)
-    arrived(q_on[5])
-    key_row(3)
-    tiles_by_chunk(4, 2)
-    arrived([share[2]])
-    loop(0, 3, lambda i: [tile(2, 0, i), tile(2, 1, i)])
-    arrived(q_on[6] + q_on[7])
-    tiles_by_chunk(6, 3)
+    unit(0, 0, 0, own=True)
+    for t in (1, 2, 3):
+        key_row(t)
+        arrived([share[t - 1]])
+        unit(t - 1, 1, 0)
+        unit(t, 0, 0)
+    arrived(q_on[5] + q_on[6] + q_on[7])
+    loop(0, 3, lambda t: [unit(t, 0, 1), unit(t, 1, 1)])
     arrived([share[3]])
-    loop(0, 4, lambda i: [tile(3, 0, i), tile(3, 1, i)])
-
-    top = jnp.max(maxes[...], axis=0, keepdims=True)
-    factor = jnp.exp2((maxes[...] - top) * log_scale)
-    total = jnp.maximum(jnp.sum(factor * totals[...], axis=0, keepdims=True), TINY)
-    near = top * log_scale + jnp.log2(total)
-    mean = jnp.sum(factor * deltas[...], axis=0, keepdims=True) / total
+    unit(3, 0, 1)
+    unit(3, 1, 1)
+    unit(3, 1, 0)
+    off = bias[...] > 0
+    top = jnp.max(jnp.where(off, -BIG, maxes[...]), axis=(0, 1), keepdims=True)
+    factor = jnp.where(off, 0.0, jnp.exp2((maxes[...] - top) * log_scale))
+    total = jnp.maximum(jnp.sum(factor * totals[...], axis=(0, 1), keepdims=True), TINY)
+    near = (top * log_scale + jnp.log2(total))[0]
+    mean = (jnp.sum(factor * deltas[...], axis=(0, 1), keepdims=True) / total)[0]
     factors[...] = factor / total
     for i in range(ZQ):
         one = pl.ds(zs[-RING8[i] % 8], 1)
@@ -228,16 +216,20 @@
 
     loop(0, CHUNKS, turn)
 
-    def attend(i):
-        at = pl.ds(pl.multiple_of(i * CQ, CQ), CQ)
-        accum = jnp.zeros((B, CQ), F32)
+    def scaled(j, at):
+        p = probs[j, :, at].astype(F32).reshape(4, B, CH) * factors[j, :, at][:, None, :]
+        return p.reshape(KC, CH)
+
+    def attend(half):
+        at = pl.ds(pl.multiple_of(half * CH, CH), CH)
+        accum = jnp.zeros((B, CH), F32)
         for j in range(CHUNKS):
-            accum += dot(vt[j], probs[j, :, at], 1, 0) * factors[j : j + 1, at]
+            accum += dot(vt[j], scaled(j, at).astype(BF16), 1, 0)
         accum = accum.astype(BF16)
-        o_send[2 * i] = accum[:, :B]
-        o_send[2 * i + 1] = accum[:, B:]
-
-    loop(0, ZQ // 2, attend)
+        for i in range(4):
+            o_send[4 * half + i] = accum[:, i * B : (i + 1) * B]
+
+    loop(0, 2, attend)
     o_copies = [copy(o_send.at[i], o_recv.at[i], line(-RING8[i])) for i in range(1, ZQ)]
     start(o_copies)
     o_recv[0] = o_send[0]
@@ -252,25 +244,27 @@
     def row_of(first):
         return jnp.concatenate([rows[pl.ds(first + zs[-RING8[i] % 8], 1), :] for i in range(ZQ)], axis=1)
 
-    maxes[...] = jnp.exp2(maxes[...] * log_scale - row_of(0))
-    deltas[0:1, :] = row_of(8)
-
-    def backward_q(i):
-        at = pl.ds(pl.multiple_of(i * CQ, CQ), CQ)
-        accum = jnp.zeros((B, CQ), F32)
+    factors[...] = jnp.where(off, 0.0, jnp.exp2(maxes[...] * log_scale - row_of(0)[None]))
+    rowdelta[...] = row_of(8)
+
+    dq_copies = {i: copy(dq_send.at[i], dq_recv.at[i], line(-RING8[i])) for i in range(1, ZQ)}
+
+    def backward_q(half):
+        at = slice(half * CH, (half + 1) * CH)
+        accum = jnp.zeros((B, CH), F32)
         for j in range(CHUNKS):
-            p = probs[j, :, at].astype(F32) * maxes[j : j + 1, at]
+            p = scaled(j, at)
             probs[j, :, at] = p.astype(BF16)
-            ds = (p * (dprobs[j, :, at] - deltas[0:1, at])).astype(BF16)
+            ds = (p * (dprobs[j, :, at] - rowdelta[:, at])).astype(BF16)
             dscores[j, :, at] = ds
             accum += dot(kt[j], ds, 1, 0)
         accum = (accum * scale).astype(BF16)
-        dq_send[2 * i] = accum[:, :B]
-        dq_send[2 * i + 1] = accum[:, B:]
-
-    dq_copies = [copy(dq_send.at[i], dq_recv.at[i], line(-RING8[i])) for i in range(1, ZQ)]
-    loop(0, ZQ // 2, backward_q)
-    start(dq_copies)
+        for i in range(4 * half, 4 * half + 4):
+            dq_send[i] = accum[:, (i - 4 * half) * B : (i - 4 * half + 1) * B]
+        start([dq_copies[i] for i in range(4 * half + 3, 4 * half - 1, -1) if i])
+
+    backward_q(1)
+    backward_q(0)
     dq_recv[0] = dq_send[0]
 
     def whole(which):
@@ -290,11 +284,13 @@
     dk_end = {b: copy(dk_turn.at[b], dk_last.at[b], row(-RING4[b])) for b in (1, 2, 3)}
     dv_end = {t: copy(dv_turn.at[t], dv_last.at[t], column(-RING4[t])) for t in (1, 2, 3)}
 
-    def key_grads(t):
+    def send_half(t):
         dk, dv = key_terms(t, 1)
         pre_send[t, 0] = dk.astype(BF16)
         pre_send[t, 1] = dv.astype(BF16)
         start([swap[t]])
+
+    def keep_half(t):
         dk, dv = key_terms(t, 0)
         part[0] = dk
         part[1] = dv
@@ -316,11 +312,15 @@
         dv_turn[t] = column_sum(t).astype(BF16)
         start([dv_end[t]])
 
-    key_grads(3)
-    key_grads(2)
-    key_grads(1)
+    send_half(3)
+    send_half(2)
+    keep_half(3)
+    send_half(1)
+    keep_half(2)
+    send_half(0)
+    keep_half(1)
     dv_pass(3)
-    key_grads(0)
+    keep_half(0)
     arrived(dk_out.values())
     turned = dk_row[0].astype(F32)
     for t in (1, 2, 3):
@@ -336,7 +336,7 @@
         weight = jnp.exp2(st_recv[zs[RING8[i]], 0, pl.ds(z, 1), :] - rows[pl.ds(z, 1), :])
         out += o_recv[i].astype(F32) * weight
     out_ref[...] = out.astype(BF16).T
-    arrived(dq_copies)
+    arrived(dq_copies.values())
     dq_ref[...] = jnp.sum(dq_recv[...].astype(F32), axis=0).astype(BF16).T
     total_v = column_sum(0)
     arrived(dv_end.values())
@@ -371,10 +371,11 @@
             pltpu.VMEM((CHUNKS, B, KC), BF16),
             pltpu.VMEM((CHUNKS, B, KC), BF16),
             pltpu.VMEM((CHUNKS, 4, NQ), F32),
-            pltpu.VMEM((CHUNKS, NQ), F32),
-            pltpu.VMEM((CHUNKS, NQ), F32),
-            pltpu.VMEM((CHUNKS, NQ), F32),
-            pltpu.VMEM((CHUNKS, NQ), F32),
+            pltpu.VMEM((CHUNKS, 4, NQ), F32),
+            pltpu.VMEM((CHUNKS, 4, NQ), F32),
+            pltpu.VMEM((CHUNKS, 4, NQ), F32),
+            pltpu.VMEM((CHUNKS, 4, NQ), F32),
+            pltpu.VMEM((1, NQ), F32),
             pltpu.VMEM((16, B), F32),
             pltpu.VMEM((CHUNKS, KC, NQ), BF16),
             pltpu.VMEM((CHUNKS, KC, NQ), F32),

time: 60.3 us -> 54.3 us (0.900)
  Pallas kernels: 59.4 us -> 53.5 us
    pallas_call x1, Pallas kernels: 58 us -> 52 us  [per_device(): pl.pallas_call(kernel, out_shape=[block] * 4, in_specs=[vmem] * 4 + [pl.B...]
where the time goes in v4:
time: 54.3 us; the launch traced here: 54.1 us
  Pallas kernels  53.5 us (99%)
  between operations  0.64 us (1%)
    pallas_call x1, Pallas kernels, per_device(): pl.pallas_call(kernel, out_shape=[block] * 4, in_specs=[vmem] * 4 + [pl.B...  52 us
    pallas_call x1, Pallas kernels, per_device(): pl.pallas_call(finish, out_shape=[block] * 4, in_specs=[vmem] * 4, out_sp...  1.46 us

profile of v4, /device:TPU:1, one launch (start us, length us, event | category | flops | bytes accessed | tf_op | source)
XLA Modules:
  0.0 54.1 jit_solution(4231952567915314251)
XLA Ops:
  0.6 52.0 %attention.1 = (bf16[128,128]{1,0:T(8,128)(2,1)}, bf16[128,128]{1,0:T(8,128)(2,1)}, bf16[128,128]{1,0:T(8,128)(2,1)}, bf16[128,128]{1,0:T(8,128)(2,1)}) custom-call(bf16[128,128]{1,0:T(8,128)(2,1)} %q_ref.1, bf16[128,128]{1,0:T(8,128)(2,1)} %k_ref.1, bf16[128,128]{1,0:T(8,128)(2,1)} %v_ref.1, bf16[128,128]{1,0:T(8,128)(2,1)} %g_ref.1, s32[256]{0:T(256)} %order_ref.1), custom_call_target="tpu_custom_call" | custom-call | tf_op jit(solution)/shard_map/attention/pallas_call | solution.py:363
  52.6 1.5 %finish.1 = (bf16[128,128]{1,0:T(8,128)(2,1)}, bf16[128,128]{1,0:T(8,128)(2,1)}, bf16[128,128]{1,0:T(8,128)(2,1)}, bf16[128,128]{1,0:T(8,128)(2,1)}) custom-call(bf16[128,128]{1,0:T(8,128)(2,1)} %get-tuple-element.8.a_ref, bf16[128,128]{1,0:T(8,128)(2,1)} %get-tuple-element.9.b_ref, bf16[128,128]{1,0:T(8,128)(2,1)} %get-tuple-element.10.c_ref, ...), custom_call_target="tpu_custom_call" | custom-call | tf_op jit(solution)/shard_map/finish/pallas_call | solution.py:408

commit v5 on v4

--- a/solution.py
+++ b/solution.py
@@ -84,6 +84,11 @@
         for one in copies:
             one.start()
             sent.append(one)
+
+    def left():
+        for one in sent:
+            one.wait_send()
+        sent.clear()
 
     def arrived(copies):
         for one in copies:
@@ -160,13 +165,6 @@
             probs[j, here, at] = p.astype(BF16)
         dprobs[j, :, at] = dp
 
-    def loop(start, stop, step):
-        def one(i, carry):
-            step(i)
-            return carry
-
-        lax.fori_loop(start, stop, one, 0)
-
     def key_row(t):
         arrived([k_col[t], k_on[t]] + v_on[t])
         start([share[t]])
@@ -185,15 +183,19 @@
     unit(0, 0, 0, own=True)
     for t in (1, 2, 3):
         key_row(t)
-        arrived([share[t - 1]])
-        unit(t - 1, 1, 0)
         unit(t, 0, 0)
+    arrived([share[0], share[1]])
+    unit(0, 1, 0)
+    unit(1, 1, 0)
     arrived(q_on[5] + q_on[6] + q_on[7])
-    loop(0, 3, lambda t: [unit(t, 0, 1), unit(t, 1, 1)])
-    arrived([share[3]])
-    unit(3, 0, 1)
-    unit(3, 1, 1)
-    unit(3, 1, 0)
+    for t in range(4):
+        unit(t, 0, 1)
+    unit(0, 1, 1)
+    unit(1, 1, 1)
+    arrived([share[2], share[3]])
+    for t in (2, 3):
+        unit(t, 1, 0)
+        unit(t, 1, 1)
     off = bias[...] > 0
     top = jnp.max(jnp.where(off, -BIG, maxes[...]), axis=(0, 1), keepdims=True)
     factor = jnp.where(off, 0.0, jnp.exp2((maxes[...] - top) * log_scale))
@@ -206,22 +208,25 @@
         st_send[0, one, :] = near[:, i * B : (i + 1) * B]
         st_send[1, one, :] = mean[:, i * B : (i + 1) * B]
     stats = [copy(st_send, st_recv.at[z], line(RING8[i])) for i in range(1, ZQ)]
+    gathered = list(sent)
+    sent.clear()
     start(stats)
     st_recv[z] = st_send[...]
 
     def turn(j):
-        t, r = j // 2, lax.rem(j, 2)
+        t, r = j // 2, j % 2
         kt[j] = chunk(t, r, 0).T
         vt[j] = chunk(t, r, 1).T
 
-    loop(0, CHUNKS, turn)
+    for j in range(CHUNKS):
+        turn(j)
 
     def scaled(j, at):
         p = probs[j, :, at].astype(F32).reshape(4, B, CH) * factors[j, :, at][:, None, :]
         return p.reshape(KC, CH)
 
     def attend(half):
-        at = pl.ds(pl.multiple_of(half * CH, CH), CH)
+        at = slice(half * CH, (half + 1) * CH)
         accum = jnp.zeros((B, CH), F32)
         for j in range(CHUNKS):
             accum += dot(vt[j], scaled(j, at).astype(BF16), 1, 0)
@@ -229,11 +234,14 @@
         for i in range(4):
             o_send[4 * half + i] = accum[:, i * B : (i + 1) * B]
 
-    loop(0, 2, attend)
+    attend(1)
+    attend(0)
     o_copies = [copy(o_send.at[i], o_recv.at[i], line(-RING8[i])) for i in range(1, ZQ)]
     start(o_copies)
     o_recv[0] = o_send[0]
 
+    for one in gathered:
+        one.wait_send()
     arrived(stats)
     nears, means = st_recv[:, 0], st_recv[:, 1]
     top = jnp.max(nears, axis=0)
@@ -249,23 +257,22 @@
 
     dq_copies = {i: copy(dq_send.at[i], dq_recv.at[i], line(-RING8[i])) for i in range(1, ZQ)}
 
-    def backward_q(half):
+    def weigh(j):
+        for half in range(2):
+            at = slice(half * CH, (half + 1) * CH)
+            p = scaled(j, at)
+            probs[j, :, at] = p.astype(BF16)
+            dscores[j, :, at] = (p * (dprobs[j, :, at] - rowdelta[:, at])).astype(BF16)
+
+    def query_grads(half):
         at = slice(half * CH, (half + 1) * CH)
         accum = jnp.zeros((B, CH), F32)
         for j in range(CHUNKS):
-            p = scaled(j, at)
-            probs[j, :, at] = p.astype(BF16)
-            ds = (p * (dprobs[j, :, at] - rowdelta[:, at])).astype(BF16)
-            dscores[j, :, at] = ds
-            accum += dot(kt[j], ds, 1, 0)
+            accum += dot(kt[j], dscores[j, :, at], 1, 0)
         accum = (accum * scale).astype(BF16)
         for i in range(4 * half, 4 * half + 4):
             dq_send[i] = accum[:, (i - 4 * half) * B : (i - 4 * half + 1) * B]
         start([dq_copies[i] for i in range(4 * half + 3, 4 * half - 1, -1) if i])
-
-    backward_q(1)
-    backward_q(0)
-    dq_recv[0] = dq_send[0]
 
     def whole(which):
         return jnp.concatenate([qg[i, which] for i in range(ZQ)], axis=1)
@@ -284,19 +291,25 @@
     dk_end = {b: copy(dk_turn.at[b], dk_last.at[b], row(-RING4[b])) for b in (1, 2, 3)}
     dv_end = {t: copy(dv_turn.at[t], dv_last.at[t], column(-RING4[t])) for t in (1, 2, 3)}
 
-    def send_half(t):
+    def send_half(t, *following):
         dk, dv = key_terms(t, 1)
+        for j in following:
+            weigh(j)
         pre_send[t, 0] = dk.astype(BF16)
         pre_send[t, 1] = dv.astype(BF16)
         start([swap[t]])
 
-    def keep_half(t):
+    def keep_half(t, *following):
         dk, dv = key_terms(t, 0)
-        part[0] = dk
-        part[1] = dv
+        for j in following:
+            weigh(j)
+        part[t, 0] = dk
+        part[t, 1] = dv
+
+    def merge(t):
         arrived([swap[t]])
-        dk_row[t] = (part[0] + pre_recv[t, 0].astype(F32)).astype(BF16)
-        dv_col[t] = (part[1] + pre_recv[t, 1].astype(F32)).astype(BF16)
+        dk_row[t] = (part[t, 0] + pre_recv[t, 0].astype(F32)).astype(BF16)
+        dv_col[t] = (part[t, 1] + pre_recv[t, 1].astype(F32)).astype(BF16)
         if t:
             start([dk_out[t]])
         start(dv_out[t])
@@ -312,24 +325,33 @@
         dv_turn[t] = column_sum(t).astype(BF16)
         start([dv_end[t]])
 
-    send_half(3)
-    send_half(2)
-    keep_half(3)
+    weigh(7)
+    send_half(3, 6)
+    keep_half(3, 5)
+    send_half(2, 4, 3, 2)
+    merge(3)
+    weigh(1)
+    weigh(0)
+    query_grads(1)
+    query_grads(0)
+    dq_recv[0] = dq_send[0]
+    keep_half(2)
+    merge(2)
     send_half(1)
-    keep_half(2)
     send_half(0)
     keep_half(1)
+    merge(1)
+    keep_half(0)
+    merge(0)
     dv_pass(3)
-    keep_half(0)
+    dv_pass(2)
+    dv_pass(1)
     arrived(dk_out.values())
     turned = dk_row[0].astype(F32)
     for t in (1, 2, 3):
         turned += dk_got[t].astype(F32)
     dk_turn[...] = turned.astype(BF16)
     start(dk_end.values())
-    dv_pass(2)
-    dv_pass(1)
-
     arrived(o_copies)
     out = jnp.zeros((B, B), F32)
     for i in range(ZQ):
@@ -338,6 +360,7 @@
     out_ref[...] = out.astype(BF16).T
     arrived(dq_copies.values())
     dq_ref[...] = jnp.sum(dq_recv[...].astype(F32), axis=0).astype(BF16).T
+    left()
     total_v = column_sum(0)
     arrived(dv_end.values())
     for t in (1, 2, 3):
@@ -348,8 +371,6 @@
     for b in (1, 2, 3):
         total_k += dk_last[b].astype(F32)
     dk_ref[...] = total_k.astype(BF16)
-    for one in sent:
-        one.wait_send()
 
 
 def finish(a_ref, b_ref, c_ref, d_ref, *outs):
@@ -388,7 +409,7 @@
             pltpu.VMEM((ZQ, B, B), BF16),
             pltpu.VMEM((4, 2, 4, B, B), BF16),
             pltpu.VMEM((4, 2, 4, B, B), BF16),
-            pltpu.VMEM((2, 4, B, B), F32),
+            pltpu.VMEM((4, 2, 4, B, B), F32),
             pltpu.VMEM((4, 4, B, B), BF16),
             pltpu.VMEM((4, 4, B, B), BF16),
             pltpu.VMEM((4, B, B), BF16),

time: 54.3 us -> 51.1 us (0.941)
  Pallas kernels: 53.5 us -> 50.1 us
    pallas_call x1, Pallas kernels: 52 us -> 48.6 us  [per_device(): pl.pallas_call(kernel, out_shape=[block] * 4, in_specs=[vmem] * 4 + [pl.B...]
where the time goes in v5:
time: 51.1 us; the launch traced here: 50.7 us
  Pallas kernels  50.1 us (98%)
  between operations  0.64 us (1%)
    pallas_call x1, Pallas kernels, per_device(): pl.pallas_call(kernel, out_shape=[block] * 4, in_specs=[vmem] * 4 + [pl.B...  48.6 us
    pallas_call x1, Pallas kernels, per_device(): pl.pallas_call(finish, out_shape=[block] * 4, in_specs=[vmem] * 4, out_sp...  1.46 us

profile of v5, /device:TPU:1, one launch (start us, length us, event | category | flops | bytes accessed | tf_op | source)
XLA Modules:
  0.0 50.7 jit_solution(12655762608332108578)
XLA Ops:
  0.6 48.6 %attention.1 = (bf16[128,128]{1,0:T(8,128)(2,1)}, bf16[128,128]{1,0:T(8,128)(2,1)}, bf16[128,128]{1,0:T(8,128)(2,1)}, bf16[128,128]{1,0:T(8,128)(2,1)}) custom-call(bf16[128,128]{1,0:T(8,128)(2,1)} %q_ref.1, bf16[128,128]{1,0:T(8,128)(2,1)} %k_ref.1, bf16[128,128]{1,0:T(8,128)(2,1)} %v_ref.1, bf16[128,128]{1,0:T(8,128)(2,1)} %g_ref.1, s32[256]{0:T(256)} %order_ref.1), custom_call_target="tpu_custom_call" | custom-call | tf_op jit(solution)/shard_map/attention/pallas_call | solution.py:384
  49.3 1.5 %finish.1 = (bf16[128,128]{1,0:T(8,128)(2,1)}, bf16[128,128]{1,0:T(8,128)(2,1)}, bf16[128,128]{1,0:T(8,128)(2,1)}, bf16[128,128]{1,0:T(8,128)(2,1)}) custom-call(bf16[128,128]{1,0:T(8,128)(2,1)} %get-tuple-element.8.a_ref, bf16[128,128]{1,0:T(8,128)(2,1)} %get-tuple-element.9.b_ref, bf16[128,128]{1,0:T(8,128)(2,1)} %get-tuple-element.10.c_ref, ...), custom_call_target="tpu_custom_call" | custom-call | tf_op jit(solution)/shard_map/finish/pallas_call | solution.py:429

commit v6 on v5

--- a/solution.py
+++ b/solution.py
@@ -120,9 +120,10 @@
     }
     share = [copy(kvg.at[t, 0], kvg.at[t, 1], sibling) for t in range(4)]
 
+    start([q_near[3], q_near[4]])
     start(k_row.values())
     start(v_col.values())
-    start(q_near.values())
+    start([q_near[1], q_near[2]])
     start(k_col.values())
     start(v_row.values())
 
@@ -181,11 +182,12 @@
     start([share[0]])
     arrived([q_near[1], q_near[2]])
     unit(0, 0, 0, own=True)
+    arrived([share[0]])
+    unit(0, 1, 0)
     for t in (1, 2, 3):
         key_row(t)
         unit(t, 0, 0)
-    arrived([share[0], share[1]])
-    unit(0, 1, 0)
+    arrived([share[1]])
     unit(1, 1, 0)
     arrived(q_on[5] + q_on[6] + q_on[7])
     for t in range(4):
@@ -210,7 +212,7 @@
     stats = [copy(st_send, st_recv.at[z], line(RING8[i])) for i in range(1, ZQ)]
     gathered = list(sent)
     sent.clear()
-    start(stats)
+    start(stats[::-1])
     st_recv[z] = st_send[...]
 
     def turn(j):
@@ -341,17 +343,17 @@
     send_half(0)
     keep_half(1)
     merge(1)
+    dv_pass(3)
     keep_half(0)
     merge(0)
-    dv_pass(3)
     dv_pass(2)
-    dv_pass(1)
     arrived(dk_out.values())
     turned = dk_row[0].astype(F32)
     for t in (1, 2, 3):
         turned += dk_got[t].astype(F32)
     dk_turn[...] = turned.astype(BF16)
-    start(dk_end.values())
+    start([dk_end[b] for b in (3, 1, 2)])
+    dv_pass(1)
     arrived(o_copies)
     out = jnp.zeros((B, B), F32)
     for i in range(ZQ):

time: 51.1 us -> 50.5 us (0.988)
  Pallas kernels: 50.1 us -> 49.1 us
    pallas_call x1, Pallas kernels: 48.6 us -> 47.6 us  [per_device(): pl.pallas_call(kernel, out_shape=[block] * 4, in_specs=[vmem] * 4 + [pl.B...]
where the time goes in v6:
time: 50.5 us; the launch traced here: 49.7 us
  Pallas kernels  49.1 us (97%)
  between operations  0.64 us (1%)
    pallas_call x1, Pallas kernels, per_device(): pl.pallas_call(kernel, out_shape=[block] * 4, in_specs=[vmem] * 4 + [pl.B...  47.6 us
    pallas_call x1, Pallas kernels, per_device(): pl.pallas_call(finish, out_shape=[block] * 4, in_specs=[vmem] * 4, out_sp...  1.46 us

profile of v6, /device:TPU:1, one launch (start us, length us, event | category | flops | bytes accessed | tf_op | source)
XLA Modules:
  0.0 49.7 jit_solution(6908057036845769730)
XLA Ops:
  0.6 47.6 %attention.1 = (bf16[128,128]{1,0:T(8,128)(2,1)}, bf16[128,128]{1,0:T(8,128)(2,1)}, bf16[128,128]{1,0:T(8,128)(2,1)}, bf16[128,128]{1,0:T(8,128)(2,1)}) custom-call(bf16[128,128]{1,0:T(8,128)(2,1)} %q_ref.1, bf16[128,128]{1,0:T(8,128)(2,1)} %k_ref.1, bf16[128,128]{1,0:T(8,128)(2,1)} %v_ref.1, bf16[128,128]{1,0:T(8,128)(2,1)} %g_ref.1, s32[256]{0:T(256)} %order_ref.1), custom_call_target="tpu_custom_call" | custom-call | tf_op jit(solution)/shard_map/attention/pallas_call | solution.py:386
  48.3 1.5 %finish.1 = (bf16[128,128]{1,0:T(8,128)(2,1)}, bf16[128,128]{1,0:T(8,128)(2,1)}, bf16[128,128]{1,0:T(8,128)(2,1)}, bf16[128,128]{1,0:T(8,128)(2,1)}) custom-call(bf16[128,128]{1,0:T(8,128)(2,1)} %get-tuple-element.8.a_ref, bf16[128,128]{1,0:T(8,128)(2,1)} %get-tuple-element.9.b_ref, bf16[128,128]{1,0:T(8,128)(2,1)} %get-tuple-element.10.c_ref, ...), custom_call_target="tpu_custom_call" | custom-call | tf_op jit(solution)/shard_map/finish/pallas_call | solution.py:431

commit v7 on v6

--- a/solution.py
+++ b/solution.py
@@ -185,10 +185,11 @@
     arrived([share[0]])
     unit(0, 1, 0)
     for t in (1, 2, 3):
+        if t == 3:
+            arrived([share[1]])
+            unit(1, 1, 0)
         key_row(t)
         unit(t, 0, 0)
-    arrived([share[1]])
-    unit(1, 1, 0)
     arrived(q_on[5] + q_on[6] + q_on[7])
     for t in range(4):
         unit(t, 0, 1)

time: 50.5 us -> 50.8 us (level)
  no operation moved by 1% of the time
where the time goes in v7:
time: 50.8 us; the launch traced here: 49.8 us
  Pallas kernels  49.1 us (97%)
  between operations  0.64 us (1%)
    pallas_call x1, Pallas kernels, per_device(): pl.pallas_call(kernel, out_shape=[block] * 4, in_specs=[vmem] * 4 + [pl.B...  47.7 us
    pallas_call x1, Pallas kernels, per_device(): pl.pallas_call(finish, out_shape=[block] * 4, in_specs=[vmem] * 4, out_sp...  1.46 us

profile of v7, /device:TPU:1, one launch (start us, length us, event | category | flops | bytes accessed | tf_op | source)
XLA Modules:
  0.0 49.8 jit_solution(13646043715049106004)
XLA Ops:
  0.6 47.7 %attention.1 = (bf16[128,128]{1,0:T(8,128)(2,1)}, bf16[128,128]{1,0:T(8,128)(2,1)}, bf16[128,128]{1,0:T(8,128)(2,1)}, bf16[128,128]{1,0:T(8,128)(2,1)}) custom-call(bf16[128,128]{1,0:T(8,128)(2,1)} %q_ref.1, bf16[128,128]{1,0:T(8,128)(2,1)} %k_ref.1, bf16[128,128]{1,0:T(8,128)(2,1)} %v_ref.1, bf16[128,128]{1,0:T(8,128)(2,1)} %g_ref.1, s32[256]{0:T(256)} %order_ref.1), custom_call_target="tpu_custom_call" | custom-call | tf_op jit(solution)/shard_map/attention/pallas_call | solution.py:387
  48.3 1.5 %finish.1 = (bf16[128,128]{1,0:T(8,128)(2,1)}, bf16[128,128]{1,0:T(8,128)(2,1)}, bf16[128,128]{1,0:T(8,128)(2,1)}, bf16[128,128]{1,0:T(8,128)(2,1)}) custom-call(bf16[128,128]{1,0:T(8,128)(2,1)} %get-tuple-element.8.a_ref, bf16[128,128]{1,0:T(8,128)(2,1)} %get-tuple-element.9.b_ref, bf16[128,128]{1,0:T(8,128)(2,1)} %get-tuple-element.10.c_ref, ...), custom_call_target="tpu_custom_call" | custom-call | tf_op jit(solution)/shard_map/finish/pallas_call | solution.py:432
